TPU v7x, 32 devices: a whole 2x2x4 slice. The times are simulated.
32 devices in a mesh: group: 4 (over z), tensor: 8 (over y, x, core).
Axes of the slice: x: 2, y: 2, z: 4, core: 2. Of those that a mesh axis runs over, the one named last changes fastest.
Arguments:
- hidden: bfloat16 [6144, 2048], P(('group', 'tensor')), may hold values from -20 to 20
- request_of: int32 [6144], P('group'), may hold values from 0 to 95, as said below
- positions: int32 [6144], P('group'), may hold values from 0 to 511, as said below
- page_table: int32 [4, 64], P('group'), may hold values from 0 to 63, each once within a row
- attn_gain: float32 [2048], replicated, may hold values from 0.5 to 1.5
- mlp_gain: float32 [2048], replicated, may hold values from 0.5 to 1.5
- wq: float32 [2048, 2048], P('group', 'tensor'), may hold values from -2 to 2
- wk: float32 [2048, 1024], P('group', 'tensor'), may hold values from -1 to 1
- wv: float32 [2048, 1024], P('group', 'tensor'), may hold values from -0.125 to 0.125
- wo: float32 [2048, 2048], P('tensor', 'group'), may hold values from -0.125 to 0.125
- w_gate: float32 [2048, 8192], P('group', 'tensor'), may hold values from -0.125 to 0.125
- w_up: float32 [2048, 8192], P('group', 'tensor'), may hold values from -0.125 to 0.125
- w_down: float32 [8192, 2048], P('tensor', 'group'), may hold values from -0.0625 to 0.0625
Outputs:
- layer_out: bfloat16 [6144, 2048], P(('group', 'tensor'))
- kv_pages: bfloat16 [256, 128, 2048], P('group', None, 'tensor')
Inputs may be any that keep to these rules, and one draw needn't show every extreme that they name: `request_of`: prompt numbers rise strictly along the token stream, starting at 0, and the last prompt of the stream has the number 6144 // 64 - 1; a prompt's rows are consecutive, and a prompt that reaches the last row of one block of 1536 rows continues at the first row of the next block. A prompt's rows have positions 0, 1, 2 and so on in order; a prompt has at most 512 rows, and one has exactly 512.
All inputs are finite; a program needn't handle non-finite values.
Results may differ from a plain program's by a relative error of at most 0.014.
Values may be sent and summed in bfloat16 or wider, within the bound.
No kernel may reach another device: no remote copies, remote signals or barrier semaphores. Data moves between devices by JAX's collectives and lax.ppermute only.
A program may use at most 128 MiB of HBM per device.

v0:
```python
import jax
import jax.numpy as jnp
from jax import lax
from jax.sharding import PartitionSpec as P

QH = 16
KVH = 8
HD = 128
PAGE = 128


rope_base = 1000000.0
norm_eps = 1e-06


def partner(value, axis, distance):
    mask = 2**distance
    pairs = [(source, source ^ mask) for source in range(lax.axis_size(axis))]
    return lax.ppermute(value, axis, pairs)


def from_behind(block, axis, distance):
    devices = range(lax.axis_size(axis))
    route = [(i - distance, i) for i in devices if i - distance in devices]
    return lax.ppermute(block, axis, route)


def rms_scale(values, gain):
    square = jnp.mean(values * values, axis=-1, keepdims=True)
    return (values * lax.rsqrt(square + norm_eps) * gain).astype(jnp.bfloat16)


def rotate(values, places):
    half_dim = values.shape[-1] // 2
    frequency = rope_base ** (-(jnp.arange(half_dim, dtype=jnp.float32) * 2.0 / values.shape[-1]))
    angle = places.astype(jnp.float32)[:, None] * frequency[None, :]
    cosine = jnp.cos(angle)[:, None, :]
    sine = jnp.sin(angle)[:, None, :]
    widened = values.astype(jnp.float32)
    first = widened[..., :half_dim]
    second = widened[..., half_dim:]
    return jnp.concatenate(
        [first * cosine - second * sine, second * cosine + first * sine], axis=-1
    ).astype(jnp.bfloat16)


def join_halves(own_part, other_part):
    even = lax.axis_index("tensor") % 2 == 0
    lower = jnp.where(even, own_part, other_part)
    upper = jnp.where(even, other_part, own_part)
    return jnp.concatenate([lower, upper], axis=-1)


def contract_rows(acts, pieces):
    return tuple((jnp.dot(acts, piece, preferred_element_type=jnp.float32) for piece in pieces))


def body(
    hidden,
    request_of,
    positions,
    page_table,
    attn_gain,
    mlp_gain,
    wq,
    wk,
    wv,
    wo,
    w_gate,
    w_up,
    w_down,
):
    tensor_count = lax.axis_size("tensor")
    rows_dev = hidden.shape[0]
    tok_group = request_of.shape[0]
    query_heads = QH // tensor_count
    key_heads = max(1, KVH // tensor_count)
    group_ratio = QH // KVH
    paired = tensor_count > KVH
    residual = lax.all_gather(hidden, "tensor", axis=0, tiled=True).astype(jnp.float32)
    normed = rms_scale(residual, attn_gain)
    query_rows = wq.astype(jnp.bfloat16)
    key_rows = wk.astype(jnp.bfloat16)
    value_rows = wv.astype(jnp.bfloat16)
    if paired:
        other_key, other_value = partner((key_rows, value_rows), "tensor", 0)
        key_rows = join_halves(key_rows, other_key)
        value_rows = join_halves(value_rows, other_value)
    query_sum, key_sum, value_sum = contract_rows(
        normed,
        (
            lax.all_gather(query_rows, "group", axis=0, tiled=True),
            lax.all_gather(key_rows, "group", axis=0, tiled=True),
            lax.all_gather(value_rows, "group", axis=0, tiled=True),
        ),
    )
    query_raw = query_sum.astype(jnp.bfloat16)
    key_raw = key_sum.astype(jnp.bfloat16)
    value_raw = value_sum.astype(jnp.bfloat16)
    queries = rotate(query_raw.reshape(tok_group, query_heads, HD), positions)
    keys = rotate(key_raw.reshape(tok_group, key_heads, HD), positions)
    values = value_raw.reshape(tok_group, key_heads, HD)
    kv_rows = jnp.stack([keys, values], axis=2)
    earlier = from_behind(kv_rows, "group", 1)
    earlier_rows = earlier.shape[0]
    all_rows = jnp.concatenate([earlier, kv_rows], axis=0)
    all_keys = jnp.repeat(all_rows[:, :, 0], group_ratio, axis=1)[:, :query_heads]
    all_values = jnp.repeat(all_rows[:, :, 1], group_ratio, axis=1)[:, :query_heads]
    first_request = request_of[0]
    first_position = positions[0]
    same_local = (request_of[:, None] == request_of[None, :]) & (
        positions[None, :] <= positions[:, None]
    )
    same_earlier = (request_of[:, None] == first_request) & (
        jnp.arange(earlier_rows)[None, :] >= earlier_rows - first_position
    )
    visible = jnp.concatenate([same_earlier, same_local], axis=1)
    scores = jnp.einsum(
        "qhd,khd->hqk", queries, all_keys, preferred_element_type=jnp.float32
    ) * HD ** (-0.5)
    scores = jnp.where(visible[None], scores, -1e30)
    row_peak = jnp.max(scores, axis=-1, keepdims=True)
    probs = jnp.where(visible[None], jnp.exp(scores - row_peak), 0.0)
    total = jnp.sum(probs, axis=-1, keepdims=True)
    mixed_heads = jnp.einsum(
        "hqk,khd->qhd", probs.astype(jnp.bfloat16), all_values, preferred_element_type=jnp.float32
    ) / jnp.transpose(total, (1, 0, 2))
    attended = mixed_heads.astype(jnp.bfloat16).reshape(tok_group, query_heads * HD)
    out_rows = wo.astype(jnp.bfloat16)
    attn_part = jnp.dot(
        attended,
        lax.all_gather(out_rows, "group", axis=1, tiled=True),
        preferred_element_type=jnp.float32,
    )
    mixed = residual + lax.psum(attn_part.astype(jnp.bfloat16), "tensor").astype(jnp.float32)
    normed_mlp = rms_scale(mixed, mlp_gain)
    gate_rows = w_gate.astype(jnp.bfloat16)
    up_rows = w_up.astype(jnp.bfloat16)
    gate_sum, up_sum = contract_rows(
        normed_mlp,
        (
            lax.all_gather(gate_rows, "group", axis=0, tiled=True),
            lax.all_gather(up_rows, "group", axis=0, tiled=True),
        ),
    )
    activation = (jax.nn.silu(gate_sum) * up_sum).astype(jnp.bfloat16)
    down_rows = w_down.astype(jnp.bfloat16)
    down_part = jnp.dot(
        activation,
        lax.all_gather(down_rows, "group", axis=1, tiled=True),
        preferred_element_type=jnp.float32,
    )
    summed = lax.psum(down_part.astype(jnp.bfloat16), "tensor").astype(jnp.float32)
    first_row = lax.axis_index("tensor") * rows_dev
    own_mixed = lax.dynamic_slice_in_dim(mixed, first_row, rows_dev, 0)
    own_summed = lax.dynamic_slice_in_dim(summed, first_row, rows_dev, 0)
    layer_out = (own_mixed + own_summed).astype(jnp.bfloat16)
    pages = page_table.shape[1]
    changed = jnp.concatenate(
        [jnp.ones((1,), jnp.int32), (request_of[1:] != request_of[:-1]).astype(jnp.int32)]
    )
    opens = jnp.maximum(changed, (positions % PAGE == 0).astype(jnp.int32))
    logical = jnp.cumsum(opens) - 1
    chosen = jnp.sum(
        jnp.where(logical[:, None] == jnp.arange(pages)[None, :], page_table, 0), axis=1
    )
    target = chosen * PAGE + positions % PAGE
    width = 2 * KVH * HD // tensor_count
    flat_rows = kv_rows.reshape(tok_group, key_heads * 2 * HD)
    offset = lax.axis_index("tensor") * width % (key_heads * 2 * HD)
    own_slice = lax.dynamic_slice_in_dim(flat_rows, offset, width, 1)
    cache = jnp.zeros((pages * PAGE, width), jnp.bfloat16).at[target].set(own_slice)
    return (layer_out, cache.reshape(pages, PAGE, width))


def solution(mesh):
    placed = (
        P(("group", "tensor"), None),
        P("group"),
        P("group"),
        P("group", None),
        P(),
        P(),
        P("group", "tensor"),
        P("group", "tensor"),
        P("group", "tensor"),
        P("tensor", "group"),
        P("group", "tensor"),
        P("group", "tensor"),
        P("tensor", "group"),
    )
    return jax.shard_map(
        body,
        mesh=mesh,
        in_specs=placed,
        out_specs=(P(("group", "tensor"), None), P("group", None, "tensor")),
        check_vma=False,
    )
```

profile of v0, /device:TPU:0, one launch (start us, length us, event | category | flops | bytes accessed | tf_op | source)
XLA Modules:
  0.0 641.3 jit_solution(17971277564374395430)
XLA Ops:
  7.2 0.0 all-gather.7.cloned.1.call-start
  7.3 0.7 all-gather.7.cloned.1.call-update
  7.9 0.0 all-gather.9.cloned.1.call-start
  8.0 1.8 convert_element_type.103
  9.8 0.0 all-gather.9.cloned.1.call-update
  9.8 0.0 all-gather.11.cloned.1.call-start
  9.8 1.8 convert_element_type.109
  11.7 0.0 all-reduce.3.cloned.1.call-start
  11.7 0.8 slice_compare_fusion
  12.6 1.2 slice.40
  13.8 1.2 slice.41
  15.0 3.3 compare_and_fusion
  18.3 1.0 convert_element_type.96
  19.3 17.4 %all_gather.25 = bf16[2048,128]{1,0:T(8,128)(2,1)S(1)} all-gather(bf16[512,128]{1,0:T(8,128)(2,1)S(1)} %convert_element_type.96), channel_id=1, replica_groups=mesh['group'=4,'tensor'=8] {'group'}, dimensions={0}, use_global_device_ids=true | all-gather | bytes 655360 | tf_op jit(solution)/shard_map/all_gather | solution.py:93
  36.6 0.1 maximum_bitcast_fusion
  36.7 0.3 reduce-window.9
  37.0 0.1 slice.55
  37.1 0.1 slice_reduce_fusion
  37.2 0.1 add_bitcast_fusion
  37.3 0.1 select_reduce_fusion
  37.5 17.0 %all_gather.26 = bf16[2048,128]{1,0:T(8,128)(2,1)} all-gather(bf16[512,128]{1,0:T(8,128)(2,1)S(1)} %convert_element_type.101), channel_id=1, replica_groups=mesh['group'=4,'tensor'=8] {'group'}, dimensions={0}, use_global_device_ids=true | all-gather | bytes 655360 | tf_op jit(solution)/shard_map/all_gather | solution.py:94
  54.4 4.3 multiply_cosine_fusion
  59.4 0.6 iota_compare_fusion.1
  60.0 1.5 broadcast_and_fusion
  61.5 3.7 pad_add_fusion
  65.3 4.4 fusion.7
  69.7 0.4 copy-done.1
  70.1 1.5 fusion.9
  71.7 2.2 fusion.28
  73.9 1.6 fusion.53
  75.6 2.2 fusion.29
  77.8 0.9 pad_maximum_fusion
  78.8 3.7 collective-permute-start
  82.5 9.8 %all-gather.9.cloned.1.call-done = bf16[2048,256]{1,0:T(8,128)(2,1)} async-done(((bf16[512,256]{1,0:T(8,128)(2,1)}), bf16[2048,256]{1,0:T(8,128)(2,1)}) %all-gather.9.cloned.1.call-update) | async-done | bytes 1048592 | tf_op jit(solution)/shard_map/all_gather | solution.py:92
  92.2 4.9 convolution_convert_fusion.2
  97.1 1.1 fusion.64
  98.2 0.5 copy.26
  98.6 1.6 copy.27
  100.3 3.0 subtract_convert_fusion
  103.3 1.4 maximum_maximum_fusion
  104.8 1.0 slice_bitcast_fusion.1
  105.8 0.4 copy.24
  106.2 22.0 %fusion.65 = f32[2,1536]{1,0:T(2,128)S(1)} fusion(pred[1536,3072]{1,0:T(8,128)(4,1)} %pad_add_fusion, bf16[3072,128]{1,0:T(8,128)(2,1)S(1)} %copy.24, bf16[1536,2,64]{2,0,1:T(8,128)(2,1)S(1)} %copy-done.10, bf16[1536,2,64]{2,0,1:T(8,128)(2,1)S(1)} %copy-done.9), kind=kOutput, calls=%fused_computation.87 | convolution fusion | flops 2464680960 | bytes 6303744 | tf_op jit(solution)/shard_map/sub | solution.py:123
  128.2 21.6 %fusion.22 = bf16[1536,2,128]{0,2,1:T(8,128)(2,1)S(1)} fusion(pred[1536,3072]{1,0:T(8,128)(4,1)} %pad_add_fusion, f32[1536,2]{0,1:T(2,128)S(1)} %bitcast.58, bf16[3072,128]{1,0:T(8,128)(2,1)} %copy-done.12, bf16[3072,128]{0,1:T(8,128)(2,1)} %get-tuple-element.6, bf16[1536,2,64]{2,0,1:T(8,128)(2,1)S(1)} %copy-done.11, bf16[1536,2,64]{2,0,1:T(8,128)(2,1)S(1)} %copy-done.9), kind=kOutput, calls=%fused_computation.28 | convolution fusion | flops 4881389568 | bytes 7876608 | tf_op jit(solution)/shard_map/hqk,khd->qhd/dot_general | solution.py:125
  149.8 0.0 all-gather.11.cloned.1.call-done
  149.9 5.9 convolution_convert_fusion
  155.8 0.0 all-gather.13.cloned.1.call-start
  155.8 1.2 convert_element_type.113
  157.1 0.0 all-gather.15.cloned.1.call-start
  157.1 2.9 convert_element_type.114
  160.0 0.0 all-gather.17.cloned.1.call-start
  160.1 1.1 convert_element_type.116
  161.2 0.0 all-reduce.5.cloned.1.call-start
  161.2 99.8 %all-reduce.3.cloned.1.call-done = bf16[1536,2048]{1,0:T(8,128)(2,1)} async-done(((bf16[1536,2048]{1,0:T(8,128)(2,1)}), bf16[1536,2048]{1,0:T(8,128)(2,1)}) %all-reduce.3.cloned.1.call-update) | async-done | bytes 6291472 | tf_op jit(solution)/shard_map/psum | solution.py:135
  261.0 11.8 %multiply_reduce_fusion = (f32[1536]{0:T(1024)S(1)}, f32[1536,2048]{1,0:T(8,128)}) fusion(bf16[1536,2048]{1,0:T(8,128)(2,1)} %all-reduce.3.cloned.1.call-done, bf16[1536,2048]{1,0:T(8,128)(2,1)} %all-gather.7.cloned.1.call-done), kind=kLoop, calls=%fused_computation.18 | loop fusion | flops 15727104 | bytes 25171968 | tf_op jit(solution)/shard_map/reduce_sum | solution.py:29
  272.9 70.6 %all-gather.13.cloned.1.call-done = bf16[2048,1024]{1,0:T(8,128)(2,1)} async-done(((bf16[512,1024]{1,0:T(8,128)(2,1)}), bf16[2048,1024]{1,0:T(8,128)(2,1)}) %all-gather.13.cloned.1.call-update) | async-done | bytes 4194320 | tf_op jit(solution)/shard_map/all_gather | solution.py:142
  343.4 13.2 %fusion.63 = f32[1536,1024]{1,0:T(8,128)} fusion(bf16[2048,1024]{1,0:T(8,128)(2,1)} %all-gather.13.cloned.1.call-done, f32[2048]{0:T(1024)S(1)} %copy-done.18, f32[1536]{0:T(1024)S(1)} %add_rsqrt_fusion, bf16[1536,2048]{1,0:T(8,128)(2,1)} %all-gather.7.cloned.1.call-done, bf16[1536,2048]{1,0:T(8,128)(2,1)} %all-reduce.3.cloned.1.call-done), kind=kOutput, calls=%fused_computation.85 | convolution fusion | flops 6461325312 | bytes 23083008 | tf_op jit(solution)/shard_map/dot_general | solution.py:55
  356.6 67.6 %all-gather.15.cloned.1.call-done = bf16[2048,1024]{1,0:T(8,128)(2,1)} async-done(((bf16[512,1024]{1,0:T(8,128)(2,1)}), bf16[2048,1024]{1,0:T(8,128)(2,1)}) %all-gather.15.cloned.1.call-update) | async-done | bytes 4194320 | tf_op jit(solution)/shard_map/all_gather | solution.py:143
  424.3 81.5 %all-gather.17.cloned.1.call-done = bf16[1024,2048]{1,0:T(8,128)(2,1)} async-done(((bf16[1024,512]{1,0:T(8,128)(2,1)}), bf16[1024,2048]{1,0:T(8,128)(2,1)}) %all-gather.17.cloned.1.call-update) | async-done | bytes 4194320 | tf_op jit(solution)/shard_map/all_gather | solution.py:150
  505.8 22.6 %convolution_convert_fusion.1 = bf16[1536,2048]{1,0:T(8,128)(2,1)} fusion(bf16[1024,2048]{1,0:T(8,128)(2,1)} %all-gather.17.cloned.1.call-done, f32[1536,1024]{1,0:T(8,128)} %fusion.63, bf16[2048,1024]{1,0:T(8,128)(2,1)} %all-gather.15.cloned.1.call-done, f32[2048]{0:T(1024)S(1)} %copy-done.18, f32[1536]{0:T(1024)S(1)} %add_rsqrt_fusion, ...), kind=kOutput, calls=%fused_computation.21 | convolution fusion | flops 12916359168 | bytes 33568768 | tf_op jit(solution)/shard_map/dot_general | solution.py:148
  528.5 1.4 copy.25
  529.9 9.9 %scatter_custom_fusion = bf16[8192,256]{1,0:T(8,128)(2,1)} fusion(s32[1536]{0:T(1024)S(1)} %get-tuple-element.14, bf16[1536,256]{1,0:T(8,128)(2,1)S(1)} %copy.25, bf16[]{:T(256)} %constant.68.clone.1), kind=kCustom, calls=%fused_computation.34 | custom fusion | bytes 4194306 | tf_op jit(solution)/shard_map/scatter | solution.py:172
  539.8 91.6 %all-reduce.5.cloned.1.call-done = bf16[1536,2048]{1,0:T(8,128)(2,1)} async-done(((bf16[1536,2048]{1,0:T(8,128)(2,1)}), bf16[1536,2048]{1,0:T(8,128)(2,1)}) %all-reduce.5.cloned.1.call-update) | async-done | bytes 6291472 | tf_op jit(solution)/shard_map/psum | solution.py:153
  631.4 2.7 add_convert_fusion
  (51 shorter events, 0.3 us)
Async XLA Ops:
  7.2 52.2 %copy-start.14 = (s32[1536]{0:T(1024)S(1)}, s32[1536]{0:T(1024)}, u32[]{:S(2)}) copy-start(s32[1536]{0:T(1024)} %param.14) | copy-start | bytes 18436
  7.2 29.5 %copy-start.15 = (s32[1536]{0:T(1024)S(1)}, s32[1536]{0:T(1024)}, u32[]{:S(2)}) copy-start(s32[1536]{0:T(1024)} %param.15) | copy-start | bytes 18436
  7.2 30.1 %copy-start.17 = (s32[1,64]{1,0:T(1,128)S(1)}, s32[1,64]{1,0:T(1,128)}, u32[]{:S(2)}) copy-start(s32[1,64]{1,0:T(1,128)} %param.16) | copy-start | bytes 772
  7.2 30.3 %copy-start.13 = (f32[512,128]{1,0:T(8,128)S(1)}, f32[512,128]{1,0:T(8,128)}, u32[]{:S(2)}) copy-start(f32[512,128]{1,0:T(8,128)} %param.21) | copy-start | bytes 786436
  7.2 58.1 %all-gather.7.cloned.1.call-start = ((), (), s32[]{:S(2)}) async-start(), calls=%async_computation | async-start | bytes 7077888 | tf_op jit(solution)/shard_map/all_gather | solution.py:80
  7.9 84.3 %all-gather.9.cloned.1.call-start = ((), (), s32[]{:S(2)}) async-start(), calls=%async_computation.1 | async-start | bytes 1310720 | tf_op jit(solution)/shard_map/all_gather | solution.py:92
  9.8 140.1 %all-gather.11.cloned.1.call-start = ((), (), s32[]{:S(2)}) async-start(), calls=%async_computation.2 | async-start | bytes 1310720 | tf_op jit(solution)/shard_map/all_gather | solution.py:132
  11.7 249.4 %all-reduce.3.cloned.1.call-start = ((), (), s32[]{:S(2)}) async-start(), calls=%async_computation.3 | async-start | bytes 12582912 | tf_op jit(solution)/shard_map/psum | solution.py:135
  61.5 8.2 %copy-start.16 = (f32[2048]{0:T(1024)S(1)}, f32[2048]{0:T(1024)}, u32[]{:S(2)}) copy-start(f32[2048]{0:T(1024)} %param.17) | copy-start | bytes 24580
  65.3 4.9 copy-start.1
  71.6 3.9 copy-start
  71.7 3.9 copy-start.2
  75.6 3.2 copy-start.5
  75.6 3.2 copy-start.7
  78.8 24.6 %collective-permute-start = (bf16[1536,1,2,128]{0,3,2,1:T(8,128)(2,1)}, bf16[1536,1,2,128]{0,3,2,1:T(8,128)(2,1)}, u32[]{:S(2)}, u32[]{:S(2)}) collective-permute-start(bf16[1536,1,2,128]{0,3,2,1:T(8,128)(2,1)} %pad_maximum_fusion), channel_id=1, source_target_pairs={{0,8},{8,16},{16,24},{1,9},{9,17},{17,25},{2,10},{10,18},{18,26},{... | collective-permute-start | bytes 2359304 | tf_op jit(solution)/shard_map/ppermute | solution.py:25
  100.2 3.1 copy-start.6
  100.3 3.1 copy-start.8
  103.3 2.9 copy-start.9
  103.3 2.9 copy-start.10
  106.1 22.1 %copy-start.12 = (bf16[3072,128]{1,0:T(8,128)(2,1)}, bf16[3072,128]{1,0:T(8,128)(2,1)S(1)}, u32[]{:S(2)}) copy-start(bf16[3072,128]{1,0:T(8,128)(2,1)S(1)} %copy.24) | copy-start | bytes 2359300
  106.2 22.1 %copy-start.11 = (bf16[1536,2,64]{2,0,1:T(8,128)(2,1)S(1)}, bf16[1536,2,64]{2,0,1:T(8,128)(2,1)}, u32[]{:S(2)}) copy-start(bf16[1536,2,64]{2,0,1:T(8,128)(2,1)} %get-tuple-element.5) | copy-start | bytes 1179652
  149.9 6.0 copy-start.3
  155.8 187.6 %all-gather.13.cloned.1.call-start = ((), (), s32[]{:S(2)}) async-start(), calls=%async_computation.4 | async-start | bytes 5242880 | tf_op jit(solution)/shard_map/all_gather | solution.py:142
  157.0 3.0 copy-start.4
  157.1 267.2 %all-gather.15.cloned.1.call-start = ((), (), s32[]{:S(2)}) async-start(), calls=%async_computation.5 | async-start | bytes 5242880 | tf_op jit(solution)/shard_map/all_gather | solution.py:143
  160.0 345.8 %all-gather.17.cloned.1.call-start = ((), (), s32[]{:S(2)}) async-start(), calls=%async_computation.6 | async-start | bytes 5242880 | tf_op jit(solution)/shard_map/all_gather | solution.py:150
  161.2 182.2 %copy-start.18 = (f32[2048]{0:T(1024)S(1)}, f32[2048]{0:T(1024)}, u32[]{:S(2)}) copy-start(f32[2048]{0:T(1024)} %param.18) | copy-start | bytes 24580
  161.2 470.2 %all-reduce.5.cloned.1.call-start = ((), (), s32[]{:S(2)}) async-start(), calls=%async_computation.7 | async-start | bytes 12582912 | tf_op jit(solution)/shard_map/psum | solution.py:153
Sparse Core Ops, SparseCore 0:
  9.9 48.2 all-gather.6
  60.3 31.8 all-gather.8
  93.8 28.7 all-gather.10
  155.9 105.0 all-reduce.2
  262.5 80.8 all-gather.12
  344.9 79.2 all-gather.14
  426.5 79.2 all-gather.16
  528.6 102.7 all-reduce.4
where the time goes:
time: 649 us; the launch traced here: 641 us
  waiting for transfers between devices  422 us (65%)
  matrix products  94.7 us (15%)
  other arithmetic  52.1 us (8%)
  blocking collectives  34.3 us (5%)
  local copies, waits for them, and re-layouts  18.9 us (3%)
  between operations  15.6 us (2%)
    psum x1, waiting for transfers between devices, body(): lax.psum(attn_part.astype(jnp.bfloat16), 'tensor').astype(jnp.float32)  99.8 us
    psum x1, waiting for transfers between devices, body(): lax.psum(down_part.astype(jnp.bfloat16), 'tensor').astype(jnp.float32)  91.6 us
    all_gather x1, waiting for transfers between devices, body(): lax.all_gather(down_rows, 'group', axis=1, tiled=True)  81.5 us
    all_gather x1, waiting for transfers between devices, body(): lax.all_gather(gate_rows, 'group', axis=0, tiled=True)  70.6 us
    all_gather x1, waiting for transfers between devices, body(): lax.all_gather(up_rows, 'group', axis=0, tiled=True)  67.6 us
    dot_general x1, matrix products, body(): jnp.dot(activation, lax.all_gather(down_rows, 'group', axis=1, tiled=True...  22.6 us
    dot_general x4, matrix products, contract_rows(): jnp.dot(acts, piece, preferred_element_type=jnp.float32)  22.5 us
    sub x1, matrix products, body(): probs = jnp.where(visible[None], jnp.exp(scores - row_peak), 0.0)  22 us
  transfers between devices with their start and end apart: 9, of which 6 were waited for; matrix products, arithmetic and copies ran while one was open for 21% of the time, Pallas kernels for 0%

commit v1 on v0

--- a/solution.py
+++ b/solution.py
@@ -1,16 +1,359 @@
+import functools
+
 import jax
 import jax.numpy as jnp
 from jax import lax
+from jax.experimental import pallas as pl
+from jax.experimental.pallas import tpu as pltpu
 from jax.sharding import PartitionSpec as P
 
 QH = 16
 KVH = 8
 HD = 128
 PAGE = 128
-
+REACH = 512
 
 rope_base = 1000000.0
 norm_eps = 1e-06
+
+F32 = jnp.float32
+BF16 = jnp.bfloat16
+
+ORDER = (0, 2, 4, 6, 1, 3, 5, 7)
+
+
+def swap(value, distance):
+    return lax.ppermute(
+        value, "tensor", [(i, i ^ distance) for i in range(lax.axis_size("tensor"))]
+    )
+
+
+def turn(value, distance):
+    count = lax.axis_size("group")
+    return lax.ppermute(value, "group", [(i, (i + distance) % count) for i in range(count)])
+
+
+def pair_swap(value):
+    return lax.ppermute(value, "group", [(i, i ^ 1) for i in range(lax.axis_size("group"))])
+
+
+def from_behind(block):
+    count = lax.axis_size("group")
+    return lax.ppermute(block, "group", [(i, i + 1) for i in range(count - 1)])
+
+
+def after(value, *others):
+    return lax.optimization_barrier((value, *others))[0]
+
+
+def rms_scale(values, gain):
+    square = jnp.mean(values * values, axis=-1, keepdims=True)
+    return (values * lax.rsqrt(square + norm_eps) * gain).astype(BF16)
+
+
+def gather_rows(own):
+    half = own.shape[0] // 2
+    by_x = swap(own, 2)
+    by_y = swap(own, 4)
+    far_low = swap(by_x[:half], 4)
+    far_high = swap(by_y[half:], 2)
+    far = jnp.concatenate([far_low, far_high], axis=0)
+    near = jnp.concatenate([own, by_x, by_y], axis=0)
+    return jnp.concatenate([near, far, swap(near, 1), swap(far, 1)], axis=0)
+
+
+def add(first, second):
+    return (first.astype(F32) + second.astype(F32)).astype(BF16)
+
+
+def scatter_sum(mine, other):
+    got = swap(other, 1)
+    total = add(mine, got)
+    rows = total.shape[0] // 4
+    width = total.shape[1] // 2
+    blocks = total.reshape(4, rows, 2 * width)
+    left, right = blocks[:, :, :width], blocks[:, :, width:]
+    left_in = swap(jnp.stack([left[1], left[3]]), 2)
+    right_in = swap(jnp.stack([right[2], right[3]]), 4)
+    left_keep = add(left[0], left_in[0])
+    left_on = add(left[2], left_in[1])
+    right_keep = add(right[0], right_in[0])
+    right_on = add(right[1], right_in[1])
+    left_last = swap(left_on, 4)
+    right_last = swap(right_on, 2)
+    return jnp.concatenate(
+        [
+            left_keep.astype(F32) + left_last.astype(F32),
+            right_keep.astype(F32) + right_last.astype(F32),
+        ],
+        axis=1,
+    )
+
+
+def project_kernel(place, x_ref, w_ref, cos_ref, sin_ref, q_ref, kv_ref):
+    raw = jnp.dot(x_ref[...], w_ref[...], preferred_element_type=F32).astype(BF16)
+    cosine = cos_ref[...]
+    sine = sin_ref[...]
+
+    def rotated(head):
+        wide = raw[:, head * HD : (head + 1) * HD].astype(F32)
+        turned = jnp.concatenate([wide[:, HD // 2 :], wide[:, : HD // 2]], axis=1)
+        return (wide * cosine + turned * sine).astype(BF16)
+
+    heads = q_ref.shape[1] // HD
+    for head in range(heads):
+        q_ref[:, head * HD : (head + 1) * HD] = rotated(head)
+    kv_ref[:, :HD] = rotated(heads)
+    kv_ref[:, HD:] = raw[:, (heads + 1) * HD :]
+
+
+def project(rows, weight, cosine, sine, places):
+    blocks = len(ORDER)
+    size = rows.shape[0] // blocks
+    depth = rows.shape[1]
+    width = weight.shape[1]
+    query_width = width - 2 * HD
+    there = lambda i, place: (place[i], 0)
+    return pl.pallas_call(
+        project_kernel,
+        grid_spec=pltpu.PrefetchScalarGridSpec(
+            num_scalar_prefetch=1,
+            grid=(blocks,),
+            in_specs=[
+                pl.BlockSpec((size, depth), lambda i, place: (i, 0)),
+                pl.BlockSpec((depth, width), lambda i, place: (0, 0)),
+                pl.BlockSpec((size, HD), there),
+                pl.BlockSpec((size, HD), there),
+            ],
+            out_specs=[
+                pl.BlockSpec((size, query_width), there),
+                pl.BlockSpec((size, 2 * HD), there),
+            ],
+        ),
+        out_shape=[
+            jax.ShapeDtypeStruct((rows.shape[0], query_width), BF16),
+            jax.ShapeDtypeStruct((rows.shape[0], 2 * HD), BF16),
+        ],
+        compiler_params=pltpu.CompilerParams(vmem_limit_bytes=32 * 1024 * 1024),
+        cost_estimate=pl.CostEstimate(
+            flops=2 * rows.shape[0] * depth * width,
+            bytes_accessed=2 * (rows.size + weight.size),
+            transcendentals=0,
+        ),
+        name="project",
+    )(places, rows, weight, cosine, sine)
+
+
+def attend_kernel(q_ref, kv_ref, pos_ref, out_ref):
+    step = pl.program_id(0)
+    size = q_ref.shape[0]
+    span = size + REACH
+    window = pl.ds(pl.multiple_of(step * size, size), span)
+    keys = kv_ref[window, :HD]
+    values = kv_ref[window, HD:]
+    row = lax.broadcasted_iota(jnp.int32, (size, span), 0)
+    column = lax.broadcasted_iota(jnp.int32, (size, span), 1)
+    back = row + REACH - column
+    visible = (back >= 0) & (back <= pos_ref[...])
+    for head in range(q_ref.shape[1] // HD):
+        query = q_ref[:, head * HD : (head + 1) * HD]
+        scores = lax.dot_general(
+            query, keys, (((1,), (1,)), ((), ())), preferred_element_type=F32
+        ) * HD ** (-0.5)
+        scores = jnp.where(visible, scores, -1e30)
+        peak = jnp.max(scores, axis=1, keepdims=True)
+        probs = jnp.exp(scores - peak)
+        total = jnp.sum(probs, axis=1, keepdims=True)
+        mixed = jnp.dot(probs.astype(BF16), values, preferred_element_type=F32)
+        out_ref[:, head * HD : (head + 1) * HD] = (mixed / total).astype(BF16)
+
+
+def attend(queries, all_kv, positions):
+    size = 256
+    rows, width = queries.shape
+    return pl.pallas_call(
+        attend_kernel,
+        grid=(rows // size,),
+        in_specs=[
+            pl.BlockSpec((size, width), lambda i: (i, 0)),
+            pl.BlockSpec(all_kv.shape, lambda i: (0, 0)),
+            pl.BlockSpec((size, 1), lambda i: (i, 0)),
+        ],
+        out_specs=pl.BlockSpec((size, width), lambda i: (i, 0)),
+        out_shape=jax.ShapeDtypeStruct((rows, width), BF16),
+        compiler_params=pltpu.CompilerParams(vmem_limit_bytes=32 * 1024 * 1024),
+        cost_estimate=pl.CostEstimate(
+            flops=4 * rows * (size + REACH) * width,
+            bytes_accessed=4 * rows * width,
+            transcendentals=rows * (size + REACH) * width // HD,
+        ),
+        name="attend",
+    )(queries, all_kv, positions[:, None])
+
+
+def mix_kernel(place, x_ref, w_ref, out_ref):
+    out_ref[...] = jnp.dot(x_ref[...], w_ref[...], preferred_element_type=F32).astype(BF16)
+
+
+def mix(attended, weight, places):
+    blocks = places.shape[0]
+    size = attended.shape[0] // len(ORDER)
+    depth, width = weight.shape
+    return pl.pallas_call(
+        mix_kernel,
+        grid_spec=pltpu.PrefetchScalarGridSpec(
+            num_scalar_prefetch=1,
+            grid=(blocks,),
+            in_specs=[
+                pl.BlockSpec((size, depth), lambda i, place: (place[i], 0)),
+                pl.BlockSpec((depth, width), lambda i, place: (0, 0)),
+            ],
+            out_specs=pl.BlockSpec((size, width), lambda i, place: (i, 0)),
+        ),
+        out_shape=jax.ShapeDtypeStruct((blocks * size, width), BF16),
+        compiler_params=pltpu.CompilerParams(vmem_limit_bytes=32 * 1024 * 1024),
+        cost_estimate=pl.CostEstimate(
+            flops=2 * blocks * size * depth * width,
+            bytes_accessed=2 * blocks * size * width,
+            transcendentals=0,
+        ),
+        name="mix",
+    )(places, attended, weight)
+
+
+def gate_kernel(x_ref, *refs):
+    pieces, out_ref = refs[:-1], refs[-1]
+    depth = x_ref.shape[1] // len(pieces)
+    both = None
+    for k, piece in enumerate(pieces):
+        part = jnp.dot(
+            x_ref[:, k * depth : (k + 1) * depth], piece[...], preferred_element_type=F32
+        )
+        both = part if both is None else both + part
+    half = both.shape[1] // 2
+    gate, up = both[:, :half], both[:, half:]
+    out_ref[...] = (gate / (1.0 + jnp.exp(-gate)) * up).astype(BF16)
+
+
+def gate_up(rows, pieces):
+    size = 256
+    count, depth = rows.shape
+    width = pieces[0].shape[1]
+    return pl.pallas_call(
+        gate_kernel,
+        grid=(count // size,),
+        in_specs=[pl.BlockSpec((size, depth), lambda i: (i, 0))]
+        + [pl.BlockSpec(piece.shape, lambda i: (0, 0)) for piece in pieces],
+        out_specs=pl.BlockSpec((size, width // 2), lambda i: (i, 0)),
+        out_shape=jax.ShapeDtypeStruct((count, width // 2), BF16),
+        compiler_params=pltpu.CompilerParams(vmem_limit_bytes=40 * 1024 * 1024),
+        cost_estimate=pl.CostEstimate(
+            flops=2 * count * depth * width,
+            bytes_accessed=2 * (count * depth + depth * width),
+            transcendentals=count * width // 2,
+        ),
+        name="gate_up",
+    )(rows, *pieces)
+
+
+def body(
+    hidden,
+    request_of,
+    positions,
+    page_table,
+    attn_gain,
+    mlp_gain,
+    wq,
+    wk,
+    wv,
+    wo,
+    w_gate,
+    w_up,
+    w_down,
+):
+    groups = lax.axis_size("group")
+    me = lax.axis_index("tensor")
+    group = lax.axis_index("group")
+    odd = group % 2 == 1
+    tok_group = request_of.shape[0]
+    depth = hidden.shape[1]
+    rows_dev = hidden.shape[0]
+    places = jnp.stack([me ^ k for k in ORDER]).astype(jnp.int32)
+
+    residual = hidden.astype(F32)
+    normed = gather_rows(rms_scale(residual, attn_gain))
+    small = jnp.concatenate([wq.astype(BF16), wk.astype(BF16), wv.astype(BF16)], axis=1)
+    qkv_weight = lax.all_gather(small, "group", axis=0, tiled=True)
+    out_weight = lax.all_gather(wo.astype(BF16), "group", axis=1, tiled=True)
+
+    ff = w_gate.shape[1] // 2
+    gate_b, up_b, down_b = w_gate.astype(BF16), w_up.astype(BF16), w_down.astype(BF16)
+    lower = jnp.concatenate([gate_b[:, :ff], up_b[:, :ff]], axis=1)
+    upper = jnp.concatenate([gate_b[:, ff:], up_b[:, ff:]], axis=1)
+    mine_in = jnp.where(odd, upper, lower)
+    other_in = jnp.where(odd, lower, upper)
+    mine_out = jnp.where(odd, down_b[ff:], down_b[:ff])
+    other_out = jnp.where(odd, down_b[:ff], down_b[ff:])
+    in_pieces = [mine_in]
+    out_pieces = [mine_out]
+    for distance in range(1, groups):
+        in_pieces.append(turn(mine_in if distance % 2 == 0 else other_in, distance))
+    for distance in range(1, groups):
+        out_pieces.append(turn(mine_out if distance % 2 == 0 else other_out, distance))
+
+    half_dim = HD // 2
+    frequency = rope_base ** (-(jnp.arange(half_dim, dtype=F32) * 2.0 / HD))
+    angle = positions.astype(F32)[:, None] * frequency[None, :]
+    cosine, sine = jnp.cos(angle), jnp.sin(angle)
+    cosine = jnp.concatenate([cosine, cosine], axis=1)
+    sine = jnp.concatenate([-sine, sine], axis=1)
+
+    queries, kv_rows = project(normed, qkv_weight, cosine, sine, places)
+    earlier = from_behind(kv_rows[-REACH:])
+    attended = attend(queries, jnp.concatenate([earlier, kv_rows], axis=0), positions)
+    four = len(ORDER) // 2
+    mixed = residual + scatter_sum(
+        mix(attended, out_weight, places[:four]), mix(attended, out_weight, places[four:])
+    )
+    normed_mlp = rms_scale(mixed, mlp_gain)
+
+    def to_turned(rows):
+        blocks = rows.reshape(rows.shape[0], groups, depth // groups)
+        picked = [
+            lax.dynamic_index_in_dim(blocks, (group - k) % groups, 1, keepdims=False)
+            for k in range(groups)
+        ]
+        return jnp.concatenate(picked, axis=1)
+
+    def mlp(rows):
+        acts = gate_up(gather_rows(to_turned(rows)), in_pieces)
+        part = jnp.concatenate(
+            [jnp.dot(acts, piece, preferred_element_type=F32).astype(BF16) for piece in out_pieces],
+            axis=1,
+        )
+        middle = part.shape[0] // 2
+        summed = scatter_sum(part[:middle], part[middle:])
+        return to_turned(summed)
+
+    other_rows = pair_swap(normed_mlp)
+    own_sum = mlp(normed_mlp)
+    other_sum = mlp(other_rows)
+    from_pair = pair_swap(other_sum.astype(BF16))
+    layer_out = (mixed + own_sum + from_pair.astype(F32)).astype(BF16)
+
+    pages = page_table.shape[1]
+    changed = jnp.concatenate(
+        [jnp.ones((1,), jnp.int32), (request_of[1:] != request_of[:-1]).astype(jnp.int32)]
+    )
+    opens = jnp.maximum(changed, (positions % PAGE == 0).astype(jnp.int32))
+    logical = jnp.cumsum(opens) - 1
+    chosen = jnp.sum(
+        jnp.where(logical[:, None] == jnp.arange(pages)[None, :], page_table, 0), axis=1
+    )
+    target = chosen * PAGE + positions % PAGE
+    width = kv_rows.shape[1]
+    cache = jnp.zeros((pages * PAGE, width), BF16).at[target].set(kv_rows)
+    return (layer_out, cache.reshape(pages, PAGE, width))
 
 
 def partner(value, axis, distance):
@@ -19,13 +362,13 @@
     return lax.ppermute(value, axis, pairs)
 
 
-def from_behind(block, axis, distance):
+def plain_from_behind(block, axis, distance):
     devices = range(lax.axis_size(axis))
     route = [(i - distance, i) for i in devices if i - distance in devices]
     return lax.ppermute(block, axis, route)
 
 
-def rms_scale(values, gain):
+def plain_rms_scale(values, gain):
     square = jnp.mean(values * values, axis=-1, keepdims=True)
     return (values * lax.rsqrt(square + norm_eps) * gain).astype(jnp.bfloat16)
 
@@ -55,7 +398,7 @@
     return tuple((jnp.dot(acts, piece, preferred_element_type=jnp.float32) for piece in pieces))
 
 
-def body(
+def plain_body(
     hidden,
     request_of,
     positions,
@@ -78,7 +421,7 @@
     group_ratio = QH // KVH
     paired = tensor_count > KVH
     residual = lax.all_gather(hidden, "tensor", axis=0, tiled=True).astype(jnp.float32)
-    normed = rms_scale(residual, attn_gain)
+    normed = plain_rms_scale(residual, attn_gain)
     query_rows = wq.astype(jnp.bfloat16)
     key_rows = wk.astype(jnp.bfloat16)
     value_rows = wv.astype(jnp.bfloat16)
@@ -101,7 +444,7 @@
     keys = rotate(key_raw.reshape(tok_group, key_heads, HD), positions)
     values = value_raw.reshape(tok_group, key_heads, HD)
     kv_rows = jnp.stack([keys, values], axis=2)
-    earlier = from_behind(kv_rows, "group", 1)
+    earlier = plain_from_behind(kv_rows, "group", 1)
     earlier_rows = earlier.shape[0]
     all_rows = jnp.concatenate([earlier, kv_rows], axis=0)
     all_keys = jnp.repeat(all_rows[:, :, 0], group_ratio, axis=1)[:, :query_heads]
@@ -133,7 +476,7 @@
         preferred_element_type=jnp.float32,
     )
     mixed = residual + lax.psum(attn_part.astype(jnp.bfloat16), "tensor").astype(jnp.float32)
-    normed_mlp = rms_scale(mixed, mlp_gain)
+    normed_mlp = plain_rms_scale(mixed, mlp_gain)
     gate_rows = w_gate.astype(jnp.bfloat16)
     up_rows = w_up.astype(jnp.bfloat16)
     gate_sum, up_sum = contract_rows(
@@ -174,6 +517,7 @@
 
 
 def solution(mesh):
+    shaped = mesh.shape["tensor"] == len(ORDER) and mesh.shape["group"] % 2 == 0
     placed = (
         P(("group", "tensor"), None),
         P("group"),
@@ -190,7 +534,7 @@
         P("tensor", "group"),
     )
     return jax.shard_map(
-        body,
+        body if shaped else plain_body,
         mesh=mesh,
         in_specs=placed,
         out_specs=(P(("group", "tensor"), None), P("group", None, "tensor")),

time: 649 us -> 473 us (0.73)
  waiting for transfers between devices: 422 us -> 151 us
  starting transfers between devices: 4.03 us -> 112 us
  matrix products: 94.7 us -> 16.5 us
  local copies, waits for them, and re-layouts: 18.9 us -> 82.5 us
  blocking collectives: 34.3 us -> 0 us
  Pallas kernels: 0 us -> 32.4 us
    all_gather x6 -> x2, waiting for transfers between devices: 230 us -> 0.71 us  [the longest x1 0.69 us: body(): qkv_weight = lax.all_gather(small, 'group', axis=0, tiled=True)]
    psum x2 -> x0, waiting for transfers between devices: 191 us -> none  [the longest x1 99.8 us: body(): lax.psum(attn_part.astype(jnp.bfloat16), 'tensor').astype(jnp.float32)]
    ppermute x1 -> x42, waiting for transfers between devices: 0.01 us -> 150 us  [the longest x33 103 us: swap(): lax.ppermute(value, 'tensor', [(i, i ^ distance) for i in range(lax.axis_...]
    ppermute x1 -> x42, starting transfers between devices: 3.7 us -> 111 us  [the longest x6 68.2 us: turn(): lax.ppermute(value, 'group', [(i, (i + distance) % count) for i in range(...]
    dot_general x7 -> x8, matrix products: 72.6 us -> 16.5 us  [mlp(): jnp.dot(acts, piece, preferred_element_type=F32).astype(BF16)]
    all_gather x2 -> x0, blocking collectives: 34.3 us -> none  [the longest x1 17.4 us: body(): lax.all_gather(key_rows, 'group', axis=0, tiled=True)]
    pallas_call x0 -> x6, Pallas kernels: none -> 32.4 us  [the longest x2 15.3 us: gate_up(): pl.pallas_call(gate_kernel, grid=(count // size,), in_specs=[pl.BlockSpec...]
    unnamed x40 -> x109, local copies, waits for them, and re-layouts: 2.6 us -> 26.6 us
  transfers between devices with their start and end apart: 9 -> 44, of which waited for: 6 -> 23; matrix products, arithmetic and copies ran while one was open for 21% -> 27% of each run, Pallas kernels for 0% -> 6%
where the time goes in v1:
time: 473 us; the launch traced here: 467 us
  waiting for transfers between devices  151 us (32%)
  starting transfers between devices  112 us (24%)
  local copies, waits for them, and re-layouts  82.5 us (17%)
  other arithmetic  57.9 us (12%)
  Pallas kernels  32.4 us (7%)
  matrix products  16.5 us (3%)
  between operations  15.2 us (3%)
    ppermute x33, waiting for transfers between devices, swap(): lax.ppermute(value, 'tensor', [(i, i ^ distance) for i in range(lax.axis_...  103 us
    ppermute x6, starting transfers between devices, turn(): lax.ppermute(value, 'group', [(i, (i + distance) % count) for i in range(...  68.2 us
    ppermute x6, waiting for transfers between devices, turn(): lax.ppermute(value, 'group', [(i, (i + distance) % count) for i in range(...  35.8 us
    ppermute x33, starting transfers between devices, swap(): lax.ppermute(value, 'tensor', [(i, i ^ distance) for i in range(lax.axis_...  27.7 us
    unnamed x109, local copies, waits for them, and re-layouts  26.6 us
    dot_general x8, matrix products, mlp(): jnp.dot(acts, piece, preferred_element_type=F32).astype(BF16)  16.5 us
    pallas_call x2, Pallas kernels, gate_up(): pl.pallas_call(gate_kernel, grid=(count // size,), in_specs=[pl.BlockSpec...  15.3 us
    convert_element_type x6, other arithmetic, add(): return (first.astype(F32) + second.astype(F32)).astype(BF16)  13.6 us
  transfers between devices with their start and end apart: 44, of which 23 were waited for; matrix products, arithmetic and copies ran while one was open for 27% of the time, Pallas kernels for 6%

profile of v1, /device:TPU:0, one launch (start us, length us, event | category | flops | bytes accessed | tf_op | source)
XLA Modules:
  0.0 466.9 jit_solution(10830767775807553651)
XLA Ops:
  12.7 2.9 collective-permute-start
  18.7 14.5 %collective-permute-done = bf16[192,2048]{1,0:T(8,128)(2,1)S(1)} collective-permute-done((bf16[192,2048]{1,0:T(8,128)(2,1)S(1)}, bf16[192,2048]{1,0:T(8,128)(2,1)S(1)}, u32[]{:S(2)}, u32[]{:S(2)}) %collective-permute-start) | collective-permute-done | bytes 786464 | tf_op jit(solution)/shard_map/ppermute | solution.py:26
  36.5 2.8 fusion.19
  43.0 7.9 %collective-permute-done.2 = bf16[96,2048]{1,0:T(8,128)(2,1)S(1)} collective-permute-done((bf16[96,2048]{1,0:T(8,128)(2,1)S(1)}, bf16[96,2048]{1,0:T(8,128)(2,1)S(1)}, u32[]{:S(2)}, u32[]{:S(2)}) %collective-permute-start.2) | collective-permute-done | bytes 393248 | tf_op jit(solution)/shard_map/ppermute | solution.py:26
  55.0 3.4 constant_dynamic-update-slice_fusion.1
  60.0 2.8 copy-done.2
  64.4 5.9 %project.1 = (bf16[1536,256]{1,0:T(8,128)(2,1)S(1)}, bf16[1536,256]{1,0:T(8,128)(2,1)S(1)}) custom-call(s32[8]{0:T(128)S(1)} %stack.58.place, bf16[1536,2048]{1,0:T(8,128)(2,1)S(1)} %copy-done.2, bf16[2048,512]{1,0:T(8,128)(2,1)S(1)} %copy-done.3, f32[1536,128]{1,0:T(8,128)S(1)} %get-tuple-element.59.cos_ref, f32[1536,128]{1,0:T(8,128)S(1)} %get-tuple-element.60.sin_ref), custom_call_target="tpu_custom_call" | custom-call | flops 3221225472 | bytes 8388608 | tf_op jit(solution)/shard_map/project/pallas_call | solution.py:117
  70.3 3.3 collective-permute-start.6
  74.0 11.2 %collective-permute-done.6 = bf16[512,256]{1,0:T(8,128)(2,1)S(1)} collective-permute-done((bf16[512,256]{1,0:T(8,128)(2,1)S(1)}, bf16[512,256]{1,0:T(8,128)(2,1)S(1)}, u32[]{:S(2)}, u32[]{:S(2)}) %collective-permute-start.6) | collective-permute-done | bytes 262176 | tf_op jit(solution)/shard_map/ppermute | solution.py:42
  85.3 6.9 %attend.1.x_ref = bf16[1536,256]{1,0:T(8,128)(2,1)S(1)} custom-call(bf16[1536,256]{1,0:T(8,128)(2,1)S(1)} %get-tuple-element.4.q_ref, bf16[2048,256]{1,0:T(8,128)(2,1)S(1)} %pad_maximum_fusion.7.kv_ref, s32[1536,1]{1,0:T(8,128)S(1)} %broadcast_in_dim.37.pos_ref), custom_call_target="tpu_custom_call" | custom-call | flops 1207959552 | bytes 1572864 | tf_op jit(solution)/shard_map/attend/pallas_call | solution.py:174
  93.5 2.1 mix.3
  95.8 2.1 mix.2
  97.9 3.4 collective-permute-done.7
  105.1 17.7 %collective-permute-done.8 = bf16[2,192,1024]{2,1,0:T(8,128)(2,1)S(1)} collective-permute-done((bf16[2,192,1024]{2,1,0:T(8,128)(2,1)S(1)}, bf16[2,192,1024]{2,1,0:T(8,128)(2,1)S(1)}, u32[]{:S(2)}, u32[]{:S(2)}) %collective-permute-start.8) | collective-permute-done | bytes 786464 | tf_op jit(solution)/shard_map/ppermute | solution.py:26
  126.1 8.0 %collective-permute-done.9 = bf16[192,1024]{1,0:T(8,128)(2,1)S(1)} collective-permute-done((bf16[192,1024]{1,0:T(8,128)(2,1)S(1)}, bf16[192,1024]{1,0:T(8,128)(2,1)S(1)}, u32[]{:S(2)}, u32[]{:S(2)}) %collective-permute-start.9) | collective-permute-done | bytes 393248 | tf_op jit(solution)/shard_map/ppermute | solution.py:26
  135.1 1.8 convert_add_fusion.6
  139.0 2.3 reshape.140
  141.3 1.6 constant_dynamic-slice_fusion.15
  147.1 7.0 %collective-permute-start.29 = (bf16[192,2048]{1,0:T(8,128)(2,1)}, bf16[192,2048]{1,0:T(8,128)(2,1)}, u32[]{:S(2)}, u32[]{:S(2)}) collective-permute-start(bf16[192,2048]{1,0:T(8,128)(2,1)} %multiply_convert_fusion), channel_id=1, source_target_pairs={{0,8},{8,0},{16,24},{24,16},{1,9},{9,1},{17,25},{25,17},{2,10},{10... | collective-permute-start | bytes 2359304 | tf_op jit(solution)/shard_map/ppermute | solution.py:37
  155.5 1.9 convert_element_type.338
  160.2 2.0 collective-permute-done.12
  163.3 6.6 %pad_maximum_fusion.3 = bf16[576,2048]{1,0:T(8,128)(2,1)} fusion(bf16[192,2048]{1,0:T(8,128)(2,1)} %collective-permute-done.13, bf16[192,2048]{1,0:T(8,128)(2,1)} %collective-permute-done.12, bf16[192,512]{1,0:T(8,128)(2,1)S(1)} %bitcast.147, bf16[192,512]{1,0:T(8,128)(2,1)S(1)} %bitcast.149, bf16[192,512]{1,0:T(8,128)(2,1)S(1)} %bitcast.151, ...), kind=kLoop, calls=%fused_computation.18 | loop fusion | flops 14155776 | bytes 4718592 | tf_op jit(solution)/shard_map/concatenate | solution.py:61
  170.0 3.0 reshape.143
  173.0 3.8 constant_dynamic-slice_fusion.7
  183.4 2.1 constant_dynamic-update-slice_fusion.12
  185.5 2.1 constant_dynamic-update-slice_fusion.11
  187.6 18.3 %collective-permute-done.14 = bf16[96,2048]{1,0:T(8,128)(2,1)S(1)} collective-permute-done((bf16[96,2048]{1,0:T(8,128)(2,1)S(1)}, bf16[96,2048]{1,0:T(8,128)(2,1)S(1)}, u32[]{:S(2)}, u32[]{:S(2)}) %collective-permute-start.14) | collective-permute-done | bytes 393248 | tf_op jit(solution)/shard_map/ppermute | solution.py:26
  206.0 7.1 %collective-permute-start.18 = (bf16[512,1024]{1,0:T(8,128)(2,1)S(1)}, bf16[512,1024]{1,0:T(8,128)(2,1)S(1)}, u32[]{:S(2)}, u32[]{:S(2)}) collective-permute-start(bf16[512,1024]{1,0:T(8,128)(2,1)S(1)} %copy-done.26), channel_id=1, source_target_pairs={{0,8},{8,16},{16,24},{24,0},{1,9},{9,17},{17,25},{25,1},{2,10},{10... | collective-permute-start | bytes 3145736 | tf_op jit(solution)/shard_map/ppermute | solution.py:33
  213.8 2.9 collective-permute-start.20
  220.1 4.9 %pad_maximum_fusion.4 = bf16[576,2048]{1,0:T(8,128)(2,1)S(1)} fusion(bf16[192,2048]{1,0:T(8,128)(2,1)S(1)} %collective-permute-done.31, bf16[192,2048]{1,0:T(8,128)(2,1)S(1)} %collective-permute-done.30, bf16[192,512]{1,0:T(8,128)(2,1)S(1)} %bitcast.139, bf16[192,512]{1,0:T(8,128)(2,1)S(1)} %bitcast.141, bf16[192,512]{1,0:T(8,128)(2,1)S(1)} %bitcast.143, ...), kind=kLoop, calls=%fused_computation.19 | loop fusion | flops 14155776 | bytes 4718592 | tf_op jit(solution)/shard_map/concatenate | solution.py:61
  225.0 2.9 collective-permute-done.32
  230.6 1.9 constant_dynamic-update-slice_fusion.8
  233.9 6.2 %collective-permute-done.18.refs_1_ = bf16[512,1024]{1,0:T(8,128)(2,1)S(1)} collective-permute-done((bf16[512,1024]{1,0:T(8,128)(2,1)S(1)}, bf16[512,1024]{1,0:T(8,128)(2,1)S(1)}, u32[]{:S(2)}, u32[]{:S(2)}) %collective-permute-start.18) | collective-permute-done | bytes 1048608 | tf_op jit(solution)/shard_map/ppermute | solution.py:33
  240.0 55.8 %collective-permute-start.21 = (bf16[512,512]{1,0:T(8,128)(2,1)}, bf16[512,512]{1,0:T(8,128)(2,1)}, u32[]{:S(2)}, u32[]{:S(2)}) collective-permute-start(bf16[512,512]{1,0:T(8,128)(2,1)} %get-tuple-element.33), channel_id=1, source_target_pairs={{0,8},{8,16},{16,24},{24,0},{1,9},{9,17},{17,25},{25,1},{2,10},{10... | collective-permute-start | bytes 1572872 | tf_op jit(solution)/shard_map/ppermute | solution.py:33
  295.8 21.6 %collective-permute-done.19.refs_2_ = bf16[512,1024]{1,0:T(8,128)(2,1)S(1)} collective-permute-done((bf16[512,1024]{1,0:T(8,128)(2,1)S(1)}, bf16[512,1024]{1,0:T(8,128)(2,1)S(1)}, u32[]{:S(2)}, u32[]{:S(2)}) %collective-permute-start.19) | collective-permute-done | bytes 1048608 | tf_op jit(solution)/shard_map/ppermute | solution.py:33
  317.4 7.8 %gate_up.2 = bf16[1536,512]{1,0:T(8,128)(2,1)S(1)} custom-call(bf16[1536,2048]{1,0:T(8,128)(2,1)S(1)} %constant_dynamic-update-slice_fusion.7.x_ref, bf16[512,1024]{1,0:T(8,128)(2,1)S(1)} %get-tuple-element.27.refs_0_, bf16[512,1024]{1,0:T(8,128)(2,1)S(1)} %collective-permute-done.18.refs_1_, bf16[512,1024]{1,0:T(8,128)(2,1)S(1)} %collective-permute-done.19.refs_2_, ...), custom_call_target="tpu_custom_call" | custom-call | flops 6442450944 | bytes 10485760 | tf_op jit(solution)/shard_map/gate_up/pallas_call | solution.py:242
  325.2 2.1 convolution_convert_fusion.7
  327.3 2.1 convolution_convert_fusion.4
  329.4 1.9 constant_dynamic-update-slice_fusion.15
  331.4 7.6 %gate_up.3 = bf16[1536,512]{1,0:T(8,128)(2,1)S(1)} custom-call(bf16[1536,2048]{1,0:T(8,128)(2,1)S(1)} %constant_dynamic-update-slice_fusion.14.x_ref, bf16[512,1024]{1,0:T(8,128)(2,1)S(1)} %get-tuple-element.27.refs_0_, bf16[512,1024]{1,0:T(8,128)(2,1)S(1)} %collective-permute-done.18.refs_1_, bf16[512,1024]{1,0:T(8,128)(2,1)S(1)} %collective-permute-done.19.refs_2_, ...), custom_call_target="tpu_custom_call" | custom-call | flops 6442450944 | bytes 10485760 | tf_op jit(solution)/shard_map/gate_up/pallas_call | solution.py:242
  339.0 2.1 convolution_convert_fusion.3
  341.0 2.1 convolution_convert_fusion
  343.1 8.0 %collective-permute-done.22 = bf16[512,512]{1,0:T(8,128)(2,1)} collective-permute-done((bf16[512,512]{1,0:T(8,128)(2,1)}, bf16[512,512]{1,0:T(8,128)(2,1)}, u32[]{:S(2)}, u32[]{:S(2)}) %collective-permute-start.22) | collective-permute-done | bytes 524320 | tf_op jit(solution)/shard_map/ppermute | solution.py:33
  351.1 2.1 convolution_convert_fusion.1
  353.2 2.1 convolution_convert_fusion.2
  356.1 2.1 convolution_convert_fusion.5
  358.1 2.1 convolution_convert_fusion.6
  360.7 2.0 slice.271
  364.7 2.5 add_convert_fusion
  367.3 5.1 %copy.62 = bf16[768,2048]{1,0:T(8,128)(2,1)} copy(bf16[768,2048]{0,1:T(8,128)(2,1)} %add_convert_fusion) | data formatting | bytes 6291456 | tf_op jit(solution)/shard_map/convert_element_type | solution.py:66
  372.4 2.1 stack.68
  378.7 5.3 %add_convert_fusion.1 = bf16[768,2048]{0,1:T(8,128)(2,1)} fusion(bf16[768,2048]{0,1:T(8,128)(2,1)} %collective-permute-done.24, bf16[1536,2048]{0,1:T(8,128)(2,1)} %copy-done.4), kind=kLoop, calls=%fused_computation.4 | loop fusion | flops 6291456 | bytes 9437184 | tf_op jit(solution)/shard_map/convert_element_type | solution.py:66
  384.0 4.7 %copy.57 = bf16[768,2048]{1,0:T(8,128)(2,1)} copy(bf16[768,2048]{0,1:T(8,128)(2,1)} %add_convert_fusion.1) | data formatting | bytes 6291456 | tf_op jit(solution)/shard_map/convert_element_type | solution.py:66
  393.3 3.9 collective-permute-done.37
  401.6 12.5 %collective-permute-done.25 = bf16[2,192,1024]{2,1,0:T(8,128)(2,1)S(1)} collective-permute-done((bf16[2,192,1024]{2,1,0:T(8,128)(2,1)S(1)}, bf16[2,192,1024]{2,1,0:T(8,128)(2,1)S(1)}, u32[]{:S(2)}, u32[]{:S(2)}) %collective-permute-start.25) | collective-permute-done | bytes 786464 | tf_op jit(solution)/shard_map/ppermute | solution.py:26
  415.5 2.6 fusion.12
  419.6 4.4 collective-permute-done.38
  426.3 2.3 reshape.145
  430.5 5.3 %collective-permute-start.41 = (bf16[192,2048]{1,0:T(8,128)(2,1)S(1)}, bf16[192,2048]{1,0:T(8,128)(2,1)}, u32[]{:S(2)}, u32[]{:S(2)}) collective-permute-start(bf16[192,2048]{1,0:T(8,128)(2,1)S(1)} %pad_maximum_fusion.20), channel_id=1, source_target_pairs={{0,8},{8,0},{16,24},{24,16},{1,9},{9,1},{17,25},{25,17},{2,10},{10... | collective-permute-start | bytes 2359304 | tf_op jit(solution)/shard_map/ppermute | solution.py:37
  435.8 9.9 %scatter_custom_fusion = bf16[8192,256]{1,0:T(8,128)(2,1)} fusion(s32[1536]{0:T(1024)S(1)} %get-tuple-element.57, bf16[1536,256]{1,0:T(8,128)(2,1)S(1)} %get-tuple-element.5, bf16[]{:T(256)} %constant.159.clone.1), kind=kCustom, calls=%fused_computation.20 | custom fusion | bytes 4194306 | tf_op jit(solution)/shard_map/scatter | solution.py:355
  445.7 2.0 convert_add_fusion.4
  449.0 3.3 reshape.142
  452.3 5.0 %constant_dynamic-slice_fusion.11 = (f32[192,1,512]{2,1,0:T(1,128)S(1)}, f32[192,1,512]{2,1,0:T(1,128)S(1)}, f32[192,1,512]{2,1,0:T(1,128)S(1)}, f32[192,1,512]{2,1,0:T(1,128)S(1)}) fusion(f32[192,4,512]{2,1,0:T(4,128)} %reshape.142, s32[]{:T(128)S(6)} %select_n.113, s32[]{:T(128)S(6)} %select_n.119, s32[]{:T(128)S(6)} %select_n.117, s32[]{:T(128)S(6)} %select_n.115), kind=kLoop, calls=%fused_computation.147 | loop fusion | bytes 3145744 | tf_op jit(solution)/shard_map/jit(dynamic_index_in_dim)/dynamic_slice | solution.py:323
  457.5 2.4 fusion.6
  (239 shorter events, 83.7 us)
Async XLA Ops:
  7.2 4.1 copy-start.5
  7.2 4.4 copy-start.34
  7.2 52.8 %all-gather.3.cloned.1.call-start = ((), (), s32[]{:S(2)}) async-start(), calls=%async_computation | async-start | bytes 2621440 | tf_op jit(solution)/shard_map/all_gather | solution.py:286
  9.2 8.7 %copy-start.33 = (s32[1536]{0:T(1024)S(1)}, s32[1536]{0:T(1024)}, u32[]{:S(2)}) copy-start(s32[1536]{0:T(1024)} %param.14) | copy-start | bytes 18436
  9.2 8.8 %copy-start.32 = (s32[1536]{0:T(1024)S(1)}, s32[1536]{0:T(1024)}, u32[]{:S(2)}) copy-start(s32[1536]{0:T(1024)} %param.15) | copy-start | bytes 18436
  11.2 81.0 %all-gather.5.cloned.1.call-start = ((), (), s32[]{:S(2)}) async-start(), calls=%async_computation.1 | async-start | bytes 1310720 | tf_op jit(solution)/shard_map/all_gather | solution.py:287
  11.3 5.9 %copy-start.30 = (f32[256,512]{1,0:T(8,128)S(1)}, f32[256,512]{1,0:T(8,128)}, u32[]{:S(2)}) copy-start(f32[256,512]{1,0:T(8,128)} %param.22) | copy-start | bytes 1572868
  12.7 23.7 %copy-start.36 = (s32[1,64]{1,0:T(1,128)S(1)}, s32[1,64]{1,0:T(1,128)}, u32[]{:S(2)}) copy-start(s32[1,64]{1,0:T(1,128)} %param.16) | copy-start | bytes 772
  12.7 20.5 %collective-permute-start = (bf16[192,2048]{1,0:T(8,128)(2,1)S(1)}, bf16[192,2048]{1,0:T(8,128)(2,1)S(1)}, u32[]{:S(2)}, u32[]{:S(2)}) collective-permute-start(bf16[192,2048]{1,0:T(8,128)(2,1)S(1)} %get-tuple-element.7), channel_id=1, source_target_pairs={{0,2},{1,3},{2,0},{3,1},{4,6},{5,7},{6,4},{7,5},{8,10},{9,11},{10,... | collective-permute-start | bytes 2359304 | tf_op jit(solution)/shard_map/ppermute | solution.py:26
  15.6 19.0 %collective-permute-start.1 = (bf16[192,2048]{1,0:T(8,128)(2,1)S(1)}, bf16[192,2048]{1,0:T(8,128)(2,1)S(1)}, u32[]{:S(2)}, u32[]{:S(2)}) collective-permute-start(bf16[192,2048]{1,0:T(8,128)(2,1)S(1)} %get-tuple-element.7), channel_id=1, source_target_pairs={{0,4},{1,5},{2,6},{3,7},{4,0},{5,1},{6,2},{7,3},{8,12},{9,13},{10,... | collective-permute-start | bytes 2359304 | tf_op jit(solution)/shard_map/ppermute | solution.py:26
  33.2 6.2 %copy-start.10 = (bf16[192,2048]{1,0:T(8,128)(2,1)}, bf16[192,2048]{1,0:T(8,128)(2,1)S(1)}, u32[]{:S(2)}) copy-start(bf16[192,2048]{1,0:T(8,128)(2,1)S(1)} %collective-permute-done) | copy-start | bytes 2359300
  36.3 18.7 %collective-permute-start.4 = (bf16[576,2048]{1,0:T(8,128)(2,1)}, bf16[576,2048]{1,0:T(8,128)(2,1)}, u32[]{:S(2)}, u32[]{:S(2)}) collective-permute-start(bf16[576,2048]{1,0:T(8,128)(2,1)} %pad_maximum_fusion.2), channel_id=1, source_target_pairs={{0,1},{1,0},{2,3},{3,2},{4,5},{5,4},{6,7},{7,6},{8,9},{9,8},{10,11... | collective-permute-start | bytes 7077896 | tf_op jit(solution)/shard_map/ppermute | solution.py:26
  39.4 11.6 %collective-permute-start.2 = (bf16[96,2048]{1,0:T(8,128)(2,1)S(1)}, bf16[96,2048]{1,0:T(8,128)(2,1)S(1)}, u32[]{:S(2)}, u32[]{:S(2)}) collective-permute-start(bf16[96,2048]{1,0:T(8,128)(2,1)S(1)} %slice.250), channel_id=1, source_target_pairs={{0,4},{1,5},{2,6},{3,7},{4,0},{5,1},{6,2},{7,3},{8,12},{9,13},{10,... | collective-permute-start | bytes 1179656 | tf_op jit(solution)/shard_map/ppermute | solution.py:26
  41.0 11.3 %collective-permute-start.3 = (bf16[96,2048]{1,0:T(8,128)(2,1)S(1)}, bf16[96,2048]{1,0:T(8,128)(2,1)S(1)}, u32[]{:S(2)}, u32[]{:S(2)}) collective-permute-start(bf16[96,2048]{1,0:T(8,128)(2,1)S(1)} %slice.251), channel_id=1, source_target_pairs={{0,2},{1,3},{2,0},{3,1},{4,6},{5,7},{6,4},{7,5},{8,10},{9,11},{10,... | collective-permute-start | bytes 1179656 | tf_op jit(solution)/shard_map/ppermute | solution.py:26
  52.4 6.0 %collective-permute-start.5 = (bf16[192,2048]{1,0:T(8,128)(2,1)S(1)}, bf16[192,2048]{1,0:T(8,128)(2,1)S(1)}, u32[]{:S(2)}, u32[]{:S(2)}) collective-permute-start(bf16[192,2048]{1,0:T(8,128)(2,1)S(1)} %pad_maximum_fusion.10), channel_id=1, source_target_pairs={{0,1},{1,0},{2,3},{3,2},{4,5},{5,4},{6,7},{7,6},{8,9},{9,8},{10,11... | collective-permute-start | bytes 2359304 | tf_op jit(solution)/shard_map/ppermute | solution.py:26
  70.3 14.9 %collective-permute-start.6 = (bf16[512,256]{1,0:T(8,128)(2,1)S(1)}, bf16[512,256]{1,0:T(8,128)(2,1)S(1)}, u32[]{:S(2)}, u32[]{:S(2)}) collective-permute-start(bf16[512,256]{1,0:T(8,128)(2,1)S(1)} %slice.201), channel_id=1, source_target_pairs={{0,8},{8,16},{16,24},{1,9},{9,17},{17,25},{2,10},{10,18},{18,26},{... | collective-permute-start | bytes 786440 | tf_op jit(solution)/shard_map/ppermute | solution.py:42
  95.6 5.7 %collective-permute-start.7 = (bf16[768,2048]{1,0:T(8,128)(2,1)S(1)}, bf16[768,2048]{1,0:T(8,128)(2,1)S(1)}, u32[]{:S(2)}, u32[]{:S(2)}) collective-permute-start(bf16[768,2048]{1,0:T(8,128)(2,1)S(1)} %mix.3), channel_id=1, source_target_pairs={{0,1},{1,0},{2,3},{3,2},{4,5},{5,4},{6,7},{7,6},{8,9},{9,8},{10,11... | collective-permute-start | bytes 9437192 | tf_op jit(solution)/shard_map/ppermute | solution.py:26
  102.9 20.6 %copy-start.7 = (bf16[768,2048]{1,0:T(8,128)(2,1)}, bf16[768,2048]{1,0:T(8,128)(2,1)S(1)}, u32[]{:S(2)}) copy-start(bf16[768,2048]{1,0:T(8,128)(2,1)S(1)} %add_convert_fusion.2) | copy-start | bytes 9437188
  103.1 19.6 %collective-permute-start.8 = (bf16[2,192,1024]{2,1,0:T(8,128)(2,1)S(1)}, bf16[2,192,1024]{2,1,0:T(8,128)(2,1)S(1)}, u32[]{:S(2)}, u32[]{:S(2)}) collective-permute-start(bf16[2,192,1024]{2,1,0:T(8,128)(2,1)S(1)} %pad_maximum_fusion.13), channel_id=1, source_target_pairs={{0,2},{1,3},{2,0},{3,1},{4,6},{5,7},{6,4},{7,5},{8,10},{9,11},{10,... | collective-permute-start | bytes 2359304 | tf_op jit(solution)/shard_map/ppermute | solution.py:26
  103.9 19.3 %collective-permute-start.10 = (bf16[2,192,1024]{2,1,0:T(8,128)(2,1)S(1)}, bf16[2,192,1024]{2,1,0:T(8,128)(2,1)S(1)}, u32[]{:S(2)}, u32[]{:S(2)}) collective-permute-start(bf16[2,192,1024]{2,1,0:T(8,128)(2,1)S(1)} %stack.66), channel_id=1, source_target_pairs={{0,4},{1,5},{2,6},{3,7},{4,0},{5,1},{6,2},{7,3},{8,12},{9,13},{10,... | collective-permute-start | bytes 2359304 | tf_op jit(solution)/shard_map/ppermute | solution.py:26
  124.1 10.0 %collective-permute-start.9 = (bf16[192,1024]{1,0:T(8,128)(2,1)S(1)}, bf16[192,1024]{1,0:T(8,128)(2,1)S(1)}, u32[]{:S(2)}, u32[]{:S(2)}) collective-permute-start(bf16[192,1024]{1,0:T(8,128)(2,1)S(1)} %get-tuple-element.22), channel_id=1, source_target_pairs={{0,4},{1,5},{2,6},{3,7},{4,0},{5,1},{6,2},{7,3},{8,12},{9,13},{10,... | collective-permute-start | bytes 1179656 | tf_op jit(solution)/shard_map/ppermute | solution.py:26
  125.3 9.8 %collective-permute-start.11 = (bf16[192,1024]{1,0:T(8,128)(2,1)S(1)}, bf16[192,1024]{1,0:T(8,128)(2,1)}, u32[]{:S(2)}, u32[]{:S(2)}) collective-permute-start(bf16[192,1024]{1,0:T(8,128)(2,1)S(1)} %get-tuple-element.23), channel_id=1, source_target_pairs={{0,2},{1,3},{2,0},{3,1},{4,6},{5,7},{6,4},{7,5},{8,10},{9,11},{10,... | collective-permute-start | bytes 1179656 | tf_op jit(solution)/shard_map/ppermute | solution.py:26
  126.1 11.8 %copy-start.35 = (f32[2048]{0:T(1024)S(1)}, f32[2048]{0:T(1024)}, u32[]{:S(2)}) copy-start(f32[2048]{0:T(1024)} %param.18) | copy-start | bytes 24580
  144.5 17.6 %collective-permute-start.12 = (bf16[192,2048]{1,0:T(8,128)(2,1)}, bf16[192,2048]{1,0:T(8,128)(2,1)}, u32[]{:S(2)}, u32[]{:S(2)}) collective-permute-start(bf16[192,2048]{1,0:T(8,128)(2,1)} %get-tuple-element.48), channel_id=1, source_target_pairs={{0,2},{1,3},{2,0},{3,1},{4,6},{5,7},{6,4},{7,5},{8,10},{9,11},{10,... | collective-permute-start | bytes 2359304 | tf_op jit(solution)/shard_map/ppermute | solution.py:26
  145.6 17.7 %collective-permute-start.13 = (bf16[192,2048]{1,0:T(8,128)(2,1)}, bf16[192,2048]{1,0:T(8,128)(2,1)}, u32[]{:S(2)}, u32[]{:S(2)}) collective-permute-start(bf16[192,2048]{1,0:T(8,128)(2,1)} %get-tuple-element.48), channel_id=1, source_target_pairs={{0,4},{1,5},{2,6},{3,7},{4,0},{5,1},{6,2},{7,3},{8,12},{9,13},{10,... | collective-permute-start | bytes 2359304 | tf_op jit(solution)/shard_map/ppermute | solution.py:26
  147.1 22.9 %collective-permute-start.29 = (bf16[192,2048]{1,0:T(8,128)(2,1)}, bf16[192,2048]{1,0:T(8,128)(2,1)}, u32[]{:S(2)}, u32[]{:S(2)}) collective-permute-start(bf16[192,2048]{1,0:T(8,128)(2,1)} %multiply_convert_fusion), channel_id=1, source_target_pairs={{0,8},{8,0},{16,24},{24,16},{1,9},{9,1},{17,25},{25,17},{2,10},{10... | collective-permute-start | bytes 2359304 | tf_op jit(solution)/shard_map/ppermute | solution.py:37
  157.6 5.7 %copy-start.19 = (bf16[192,1,512]{2,0,1:T(8,128)(2,1)S(1)}, bf16[192,1,512]{2,0,1:T(8,128)(2,1)}, u32[]{:S(2)}) copy-start(bf16[192,1,512]{2,0,1:T(8,128)(2,1)} %copy-done.18) | copy-start | bytes 589828
  157.6 5.7 %copy-start.21 = (bf16[192,1,512]{2,0,1:T(8,128)(2,1)S(1)}, bf16[192,1,512]{2,0,1:T(8,128)(2,1)}, u32[]{:S(2)}) copy-start(bf16[192,1,512]{2,0,1:T(8,128)(2,1)} %copy-done.20) | copy-start | bytes 589828
  157.6 5.7 %copy-start.23 = (bf16[192,1,512]{2,0,1:T(8,128)(2,1)S(1)}, bf16[192,1,512]{2,0,1:T(8,128)(2,1)}, u32[]{:S(2)}) copy-start(bf16[192,1,512]{2,0,1:T(8,128)(2,1)} %copy-done.22) | copy-start | bytes 589828
  157.6 5.7 %copy-start.25 = (bf16[192,1,512]{2,0,1:T(8,128)(2,1)S(1)}, bf16[192,1,512]{2,0,1:T(8,128)(2,1)}, u32[]{:S(2)}) copy-start(bf16[192,1,512]{2,0,1:T(8,128)(2,1)} %copy-done.24) | copy-start | bytes 589828
  170.0 59.1 %collective-permute-start.16 = (bf16[576,2048]{1,0:T(8,128)(2,1)}, bf16[576,2048]{1,0:T(8,128)(2,1)}, u32[]{:S(2)}, u32[]{:S(2)}) collective-permute-start(bf16[576,2048]{1,0:T(8,128)(2,1)} %pad_maximum_fusion.3), channel_id=1, source_target_pairs={{0,1},{1,0},{2,3},{3,2},{4,5},{5,4},{6,7},{7,6},{8,9},{9,8},{10,11... | collective-permute-start | bytes 7077896 | tf_op jit(solution)/shard_map/ppermute | solution.py:26
  176.9 29.0 %copy-start.26 = (bf16[512,1024]{1,0:T(8,128)(2,1)S(1)}, bf16[512,1024]{1,0:T(8,128)(2,1)}, u32[]{:S(2)}) copy-start(bf16[512,1024]{1,0:T(8,128)(2,1)} %get-tuple-element.26) | copy-start | bytes 3145732
  177.1 40.4 %collective-permute-start.30 = (bf16[192,2048]{1,0:T(8,128)(2,1)S(1)}, bf16[192,2048]{1,0:T(8,128)(2,1)S(1)}, u32[]{:S(2)}, u32[]{:S(2)}) collective-permute-start(bf16[192,2048]{1,0:T(8,128)(2,1)S(1)} %get-tuple-element.42), channel_id=1, source_target_pairs={{0,2},{1,3},{2,0},{3,1},{4,6},{5,7},{6,4},{7,5},{8,10},{9,11},{10,... | collective-permute-start | bytes 2359304 | tf_op jit(solution)/shard_map/ppermute | solution.py:26
  177.9 40.6 %collective-permute-start.31 = (bf16[192,2048]{1,0:T(8,128)(2,1)S(1)}, bf16[192,2048]{1,0:T(8,128)(2,1)S(1)}, u32[]{:S(2)}, u32[]{:S(2)}) collective-permute-start(bf16[192,2048]{1,0:T(8,128)(2,1)S(1)} %get-tuple-element.42), channel_id=1, source_target_pairs={{0,4},{1,5},{2,6},{3,7},{4,0},{5,1},{6,2},{7,3},{8,12},{9,13},{10,... | collective-permute-start | bytes 2359304 | tf_op jit(solution)/shard_map/ppermute | solution.py:26
  180.1 25.9 %collective-permute-start.14 = (bf16[96,2048]{1,0:T(8,128)(2,1)S(1)}, bf16[96,2048]{1,0:T(8,128)(2,1)S(1)}, u32[]{:S(2)}, u32[]{:S(2)}) collective-permute-start(bf16[96,2048]{1,0:T(8,128)(2,1)S(1)} %slice.262), channel_id=1, source_target_pairs={{0,4},{1,5},{2,6},{3,7},{4,0},{5,1},{6,2},{7,3},{8,12},{9,13},{10,... | collective-permute-start | bytes 1179656 | tf_op jit(solution)/shard_map/ppermute | solution.py:26
  182.0 31.8 %collective-permute-start.15 = (bf16[96,2048]{1,0:T(8,128)(2,1)S(1)}, bf16[96,2048]{1,0:T(8,128)(2,1)S(1)}, u32[]{:S(2)}, u32[]{:S(2)}) collective-permute-start(bf16[96,2048]{1,0:T(8,128)(2,1)S(1)} %slice.263), channel_id=1, source_target_pairs={{0,2},{1,3},{2,0},{3,1},{4,6},{5,7},{6,4},{7,5},{8,10},{9,11},{10,... | collective-permute-start | bytes 1179656 | tf_op jit(solution)/shard_map/ppermute | solution.py:26
  206.0 34.1 %collective-permute-start.18 = (bf16[512,1024]{1,0:T(8,128)(2,1)S(1)}, bf16[512,1024]{1,0:T(8,128)(2,1)S(1)}, u32[]{:S(2)}, u32[]{:S(2)}) collective-permute-start(bf16[512,1024]{1,0:T(8,128)(2,1)S(1)} %copy-done.26), channel_id=1, source_target_pairs={{0,8},{8,16},{16,24},{24,0},{1,9},{9,17},{17,25},{25,1},{2,10},{10... | collective-permute-start | bytes 3145736 | tf_op jit(solution)/shard_map/ppermute | solution.py:33
  213.8 103.6 %collective-permute-start.20 = (bf16[512,1024]{1,0:T(8,128)(2,1)S(1)}, bf16[512,1024]{1,0:T(8,128)(2,1)S(1)}, u32[]{:S(2)}, u32[]{:S(2)}) collective-permute-start(bf16[512,1024]{1,0:T(8,128)(2,1)S(1)} %copy-done.26), channel_id=1, source_target_pairs={{0,24},{8,0},{16,8},{24,16},{1,25},{9,1},{17,9},{25,17},{2,26},{10... | collective-permute-start | bytes 3145736 | tf_op jit(solution)/shard_map/ppermute | solution.py:33
  217.6 10.2 %collective-permute-start.32 = (bf16[96,2048]{1,0:T(8,128)(2,1)S(1)}, bf16[96,2048]{1,0:T(8,128)(2,1)S(1)}, u32[]{:S(2)}, u32[]{:S(2)}) collective-permute-start(bf16[96,2048]{1,0:T(8,128)(2,1)S(1)} %slice.282), channel_id=1, source_target_pairs={{0,4},{1,5},{2,6},{3,7},{4,0},{5,1},{6,2},{7,3},{8,12},{9,13},{10,... | collective-permute-start | bytes 1179656 | tf_op jit(solution)/shard_map/ppermute | solution.py:26
  218.5 12.1 %slice-start = ((s8[6291456]{0:T(1024)(128)(4,1)}), s8[4194304]{0:T(1024)(128)(4,1)S(1)}, s32[]{:S(2)}) async-start(s8[6291456]{0:T(1024)(128)(4,1)} %bitcast.123), calls=%async_computation.2 | async-start | bytes 8388608
  218.5 10.5 %collective-permute-start.33 = (bf16[96,2048]{1,0:T(8,128)(2,1)S(1)}, bf16[96,2048]{1,0:T(8,128)(2,1)S(1)}, u32[]{:S(2)}, u32[]{:S(2)}) collective-permute-start(bf16[96,2048]{1,0:T(8,128)(2,1)S(1)} %slice.283), channel_id=1, source_target_pairs={{0,2},{1,3},{2,0},{3,1},{4,6},{5,7},{6,4},{7,5},{8,10},{9,11},{10,... | collective-permute-start | bytes 1179656 | tf_op jit(solution)/shard_map/ppermute | solution.py:26
  220.0 10.6 %slice-start.1 = ((s8[6291456]{0:T(1024)(128)(4,1)}), s8[2097152]{0:T(1024)(128)(4,1)S(1)}, s32[]{:S(2)}) async-start(s8[6291456]{0:T(1024)(128)(4,1)} %bitcast.123), calls=%async_computation.3 | async-start | bytes 4194304
  227.8 89.6 %collective-permute-start.19 = (bf16[512,1024]{1,0:T(8,128)(2,1)S(1)}, bf16[512,1024]{1,0:T(8,128)(2,1)S(1)}, u32[]{:S(2)}, u32[]{:S(2)}) collective-permute-start(bf16[512,1024]{1,0:T(8,128)(2,1)S(1)} %get-tuple-element.27.refs_0_), channel_id=1, source_target_pairs={{0,16},{8,24},{16,0},{24,8},{1,17},{9,25},{17,1},{25,9},{2,18},{10... | collective-permute-start | bytes 3145736 | tf_op jit(solution)/shard_map/ppermute | solution.py:33
  229.1 3.5 collective-permute-start.17
  229.1 100.3 %collective-permute-start.34 = (bf16[576,2048]{1,0:T(8,128)(2,1)S(1)}, bf16[576,2048]{1,0:T(8,128)(2,1)}, u32[]{:S(2)}, u32[]{:S(2)}) collective-permute-start(bf16[576,2048]{1,0:T(8,128)(2,1)S(1)} %pad_maximum_fusion.4), channel_id=1, source_target_pairs={{0,1},{1,0},{2,3},{3,2},{4,5},{5,4},{6,7},{7,6},{8,9},{9,8},{10,11... | collective-permute-start | bytes 7077896 | tf_op jit(solution)/shard_map/ppermute | solution.py:26
  232.6 94.7 %collective-permute-start.23 = (bf16[512,512]{1,0:T(8,128)(2,1)}, bf16[512,512]{1,0:T(8,128)(2,1)}, u32[]{:S(2)}, u32[]{:S(2)}) collective-permute-start(bf16[512,512]{1,0:T(8,128)(2,1)} %get-tuple-element.33), channel_id=1, source_target_pairs={{0,24},{8,0},{16,8},{24,16},{1,25},{9,1},{17,9},{25,17},{2,26},{10... | collective-permute-start | bytes 1572872 | tf_op jit(solution)/shard_map/ppermute | solution.py:33
  240.0 113.2 %collective-permute-start.21 = (bf16[512,512]{1,0:T(8,128)(2,1)}, bf16[512,512]{1,0:T(8,128)(2,1)}, u32[]{:S(2)}, u32[]{:S(2)}) collective-permute-start(bf16[512,512]{1,0:T(8,128)(2,1)} %get-tuple-element.33), channel_id=1, source_target_pairs={{0,8},{8,16},{16,24},{24,0},{1,9},{9,17},{17,25},{25,1},{2,10},{10... | collective-permute-start | bytes 1572872 | tf_op jit(solution)/shard_map/ppermute | solution.py:33
  317.4 33.7 %collective-permute-start.22 = (bf16[512,512]{1,0:T(8,128)(2,1)}, bf16[512,512]{1,0:T(8,128)(2,1)}, u32[]{:S(2)}, u32[]{:S(2)}) collective-permute-start(bf16[512,512]{1,0:T(8,128)(2,1)} %get-tuple-element.32), channel_id=1, source_target_pairs={{0,16},{8,24},{16,0},{24,8},{1,17},{9,25},{17,1},{25,9},{2,18},{10... | collective-permute-start | bytes 1572872 | tf_op jit(solution)/shard_map/ppermute | solution.py:33
  317.4 13.9 %collective-permute-start.35 = (bf16[192,2048]{1,0:T(8,128)(2,1)}, bf16[192,2048]{1,0:T(8,128)(2,1)S(1)}, u32[]{:S(2)}, u32[]{:S(2)}) collective-permute-start(bf16[192,2048]{1,0:T(8,128)(2,1)} %pad_maximum_fusion.17), channel_id=1, source_target_pairs={{0,1},{1,0},{2,3},{3,2},{4,5},{5,4},{6,7},{7,6},{8,9},{9,8},{10,11... | collective-permute-start | bytes 2359304 | tf_op jit(solution)/shard_map/ppermute | solution.py:26
  356.0 8.8 %collective-permute-start.36 = (bf16[768,2048]{0,1:T(8,128)(2,1)S(1)}, bf16[768,2048]{0,1:T(8,128)(2,1)S(1)}, u32[]{:S(2)}, u32[]{:S(2)}) collective-permute-start(bf16[768,2048]{0,1:T(8,128)(2,1)S(1)} %slice.285), channel_id=1, source_target_pairs={{0,1},{1,0},{2,3},{3,2},{4,5},{5,4},{6,7},{7,6},{8,9},{9,8},{10,11... | collective-permute-start | bytes 9437192 | tf_op jit(solution)/shard_map/ppermute | solution.py:26
  364.2 14.5 %collective-permute-start.24 = (bf16[768,2048]{0,1:T(8,128)(2,1)}, bf16[768,2048]{0,1:T(8,128)(2,1)}, u32[]{:S(2)}, u32[]{:S(2)}) collective-permute-start(bf16[768,2048]{0,1:T(8,128)(2,1)} %slice.271), channel_id=1, source_target_pairs={{0,1},{1,0},{2,3},{3,2},{4,5},{5,4},{6,7},{7,6},{8,9},{9,8},{10,11... | collective-permute-start | bytes 9437192 | tf_op jit(solution)/shard_map/ppermute | solution.py:26
  376.6 20.6 %collective-permute-start.37 = (bf16[2,192,1024]{2,1,0:T(8,128)(2,1)}, bf16[2,192,1024]{2,1,0:T(8,128)(2,1)S(1)}, u32[]{:S(2)}, u32[]{:S(2)}) collective-permute-start(bf16[2,192,1024]{2,1,0:T(8,128)(2,1)} %pad_maximum_fusion.19), channel_id=1, source_target_pairs={{0,2},{1,3},{2,0},{3,1},{4,6},{5,7},{6,4},{7,5},{8,10},{9,11},{10,... | collective-permute-start | bytes 2359304 | tf_op jit(solution)/shard_map/ppermute | solution.py:26
  378.0 20.8 %collective-permute-start.39 = (bf16[2,192,1024]{2,1,0:T(8,128)(2,1)}, bf16[2,192,1024]{2,1,0:T(8,128)(2,1)}, u32[]{:S(2)}, u32[]{:S(2)}) collective-permute-start(bf16[2,192,1024]{2,1,0:T(8,128)(2,1)} %stack.68), channel_id=1, source_target_pairs={{0,4},{1,5},{2,6},{3,7},{4,0},{5,1},{6,2},{7,3},{8,12},{9,13},{10,... | collective-permute-start | bytes 2359304 | tf_op jit(solution)/shard_map/ppermute | solution.py:26
  388.7 10.0 %copy-start.6 = (bf16[768,2048]{1,0:T(8,128)(2,1)S(1)}, bf16[768,2048]{1,0:T(8,128)(2,1)}, u32[]{:S(2)}) copy-start(bf16[768,2048]{1,0:T(8,128)(2,1)} %copy.62) | copy-start | bytes 9437188
  391.3 22.7 %collective-permute-start.25 = (bf16[2,192,1024]{2,1,0:T(8,128)(2,1)S(1)}, bf16[2,192,1024]{2,1,0:T(8,128)(2,1)S(1)}, u32[]{:S(2)}, u32[]{:S(2)}) collective-permute-start(bf16[2,192,1024]{2,1,0:T(8,128)(2,1)S(1)} %pad_maximum_fusion.16), channel_id=1, source_target_pairs={{0,2},{1,3},{2,0},{3,1},{4,6},{5,7},{6,4},{7,5},{8,10},{9,11},{10,... | collective-permute-start | bytes 2359304 | tf_op jit(solution)/shard_map/ppermute | solution.py:26
  392.1 23.4 %collective-permute-start.27 = (bf16[2,192,1024]{2,1,0:T(8,128)(2,1)S(1)}, bf16[2,192,1024]{2,1,0:T(8,128)(2,1)S(1)}, u32[]{:S(2)}, u32[]{:S(2)}) collective-permute-start(bf16[2,192,1024]{2,1,0:T(8,128)(2,1)S(1)} %stack.67), channel_id=1, source_target_pairs={{0,4},{1,5},{2,6},{3,7},{4,0},{5,1},{6,2},{7,3},{8,12},{9,13},{10,... | collective-permute-start | bytes 2359304 | tf_op jit(solution)/shard_map/ppermute | solution.py:26
  400.1 23.9 %collective-permute-start.38 = (bf16[192,1024]{1,0:T(8,128)(2,1)S(1)}, bf16[192,1024]{1,0:T(8,128)(2,1)S(1)}, u32[]{:S(2)}, u32[]{:S(2)}) collective-permute-start(bf16[192,1024]{1,0:T(8,128)(2,1)S(1)} %get-tuple-element.10), channel_id=1, source_target_pairs={{0,4},{1,5},{2,6},{3,7},{4,0},{5,1},{6,2},{7,3},{8,12},{9,13},{10,... | collective-permute-start | bytes 1179656 | tf_op jit(solution)/shard_map/ppermute | solution.py:26
  400.9 23.1 %collective-permute-start.40 = (bf16[192,1024]{1,0:T(8,128)(2,1)S(1)}, bf16[192,1024]{1,0:T(8,128)(2,1)S(1)}, u32[]{:S(2)}, u32[]{:S(2)}) collective-permute-start(bf16[192,1024]{1,0:T(8,128)(2,1)S(1)} %get-tuple-element.11), channel_id=1, source_target_pairs={{0,2},{1,3},{2,0},{3,1},{4,6},{5,7},{6,4},{7,5},{8,10},{9,11},{10,... | collective-permute-start | bytes 1179656 | tf_op jit(solution)/shard_map/ppermute | solution.py:26
  414.1 9.9 %copy-start.28 = (bf16[2,192,1024]{2,1,0:T(8,128)(2,1)}, bf16[2,192,1024]{2,1,0:T(8,128)(2,1)S(1)}, u32[]{:S(2)}) copy-start(bf16[2,192,1024]{2,1,0:T(8,128)(2,1)S(1)} %collective-permute-done.25) | copy-start | bytes 2359300
  415.5 9.9 %copy-start.29 = (bf16[2,192,1024]{2,1,0:T(8,128)(2,1)}, bf16[2,192,1024]{2,1,0:T(8,128)(2,1)S(1)}, u32[]{:S(2)}) copy-start(bf16[2,192,1024]{2,1,0:T(8,128)(2,1)S(1)} %collective-permute-done.27) | copy-start | bytes 2359300
  418.1 27.6 %collective-permute-start.26 = (bf16[192,1024]{1,0:T(8,128)(2,1)}, bf16[192,1024]{1,0:T(8,128)(2,1)}, u32[]{:S(2)}, u32[]{:S(2)}) collective-permute-start(bf16[192,1024]{1,0:T(8,128)(2,1)} %get-tuple-element.16), channel_id=1, source_target_pairs={{0,4},{1,5},{2,6},{3,7},{4,0},{5,1},{6,2},{7,3},{8,12},{9,13},{10,... | collective-permute-start | bytes 1179656 | tf_op jit(solution)/shard_map/ppermute | solution.py:26
  418.8 26.9 %collective-permute-start.28 = (bf16[192,1024]{1,0:T(8,128)(2,1)}, bf16[192,1024]{1,0:T(8,128)(2,1)}, u32[]{:S(2)}, u32[]{:S(2)}) collective-permute-start(bf16[192,1024]{1,0:T(8,128)(2,1)} %get-tuple-element.17), channel_id=1, source_target_pairs={{0,2},{1,3},{2,0},{3,1},{4,6},{5,7},{6,4},{7,5},{8,10},{9,11},{10,... | collective-permute-start | bytes 1179656 | tf_op jit(solution)/shard_map/ppermute | solution.py:26
  430.5 27.0 %collective-permute-start.41 = (bf16[192,2048]{1,0:T(8,128)(2,1)S(1)}, bf16[192,2048]{1,0:T(8,128)(2,1)}, u32[]{:S(2)}, u32[]{:S(2)}) collective-permute-start(bf16[192,2048]{1,0:T(8,128)(2,1)S(1)} %pad_maximum_fusion.20), channel_id=1, source_target_pairs={{0,8},{8,0},{16,24},{24,16},{1,9},{9,1},{17,25},{25,17},{2,10},{10... | collective-permute-start | bytes 2359304 | tf_op jit(solution)/shard_map/ppermute | solution.py:37
  452.3 5.2 %copy-start.9 = (f32[192,1024]{1,0:T(8,128)S(1)}, f32[192,1024]{1,0:T(8,128)}, u32[]{:S(2)}) copy-start(f32[192,1024]{1,0:T(8,128)} %copy-done.8) | copy-start | bytes 2359300
  (19 other events, 42.2 us)
Sparse Core Ops, SparseCore 0:
  11.4 48.6 all-gather.2
  61.6 29.3 all-gather.4

commit v2 on v0

--- a/solution.py
+++ b/solution.py
@@ -1,16 +1,442 @@
+import functools
+
 import jax
 import jax.numpy as jnp
 from jax import lax
+from jax.experimental import pallas as pl
+from jax.experimental.pallas import tpu as pltpu
 from jax.sharding import PartitionSpec as P
 
 QH = 16
 KVH = 8
 HD = 128
 PAGE = 128
-
+REACH = 512
 
 rope_base = 1000000.0
 norm_eps = 1e-06
+
+F32 = jnp.float32
+BF16 = jnp.bfloat16
+
+ORDER = (2, 6, 4, 0, 3, 7, 5, 1)
+
+
+def swap(value, distance):
+    return lax.ppermute(
+        value, "tensor", [(i, i ^ distance) for i in range(lax.axis_size("tensor"))]
+    )
+
+
+def turn(value, distance):
+    count = lax.axis_size("group")
+    return lax.ppermute(value, "group", [(i, (i + distance) % count) for i in range(count)])
+
+
+def pair_swap(value):
+    return lax.ppermute(value, "group", [(i, i ^ 1) for i in range(lax.axis_size("group"))])
+
+
+def from_behind(block):
+    count = lax.axis_size("group")
+    return lax.ppermute(block, "group", [(i, i + 1) for i in range(count - 1)])
+
+
+def tied(*values):
+    return lax.optimization_barrier(values)
+
+
+def after(value, *others):
+    return lax.optimization_barrier((value, *others))[0]
+
+
+def rms_scale(values, gain):
+    square = jnp.mean(values * values, axis=-1, keepdims=True)
+    return (values * lax.rsqrt(square + norm_eps) * gain).astype(BF16)
+
+
+def gather_first(own):
+    return swap(own, 2), swap(own, 4)
+
+
+def gather_far(firsts):
+    by_x, by_y = firsts
+    half = by_x.shape[0] // 2
+    return swap(by_x[:half], 4), swap(by_y[half:], 2)
+
+
+def near_blocks(own, firsts, far):
+    return [firsts[0], far[0], far[1], firsts[1], own]
+
+
+def over(near):
+    return [swap(block, 1) for block in near]
+
+
+def wide_sum(*terms):
+    total = terms[0].astype(F32)
+    for term in terms[1:]:
+        total = total + term.astype(F32)
+    return total
+
+
+def scatter_sum(mine, other):
+    got_left, got_right = (swap(half, 1) for half in other)
+    left, right = mine
+    rows = left.shape[0] // 4
+    two, three = 2 * rows, 3 * rows
+    left_in = swap(wide_sum(left[:two], got_left[:two]).astype(BF16), 2)
+    right_in = swap(wide_sum(right[rows:three], got_right[rows:three]).astype(BF16), 4)
+    left_on = wide_sum(left[two:three], got_left[two:three], left_in[rows:]).astype(BF16)
+    right_on = wide_sum(right[:rows], got_right[:rows], right_in[:rows]).astype(BF16)
+    left_last = swap(left_on, 4)
+    right_last = swap(right_on, 2)
+    return (
+        wide_sum(left[three:], got_left[three:], left_in[:rows], left_last),
+        wide_sum(right[three:], got_right[three:], right_in[rows:], right_last),
+    )
+
+
+def project_kernel(blocks, places, *refs):
+    rows, (w_ref, cos_ref, sin_ref, q_ref, kv_ref) = refs[:blocks], refs[blocks:]
+    heads = q_ref.shape[1] // HD
+    for b, block in enumerate(rows):
+        size = block.shape[0]
+        raw = jnp.dot(block[...], w_ref[...], preferred_element_type=F32).astype(BF16)
+        here = pl.ds(pl.multiple_of(places[b], 32), size)
+        cosine = cos_ref[here, :]
+        sine = sin_ref[here, :]
+
+        def rotated(head):
+            wide = raw[:, head * HD : (head + 1) * HD].astype(F32)
+            turned = jnp.concatenate([wide[:, HD // 2 :], wide[:, : HD // 2]], axis=1)
+            return (wide * cosine + turned * sine).astype(BF16)
+
+        for head in range(heads):
+            q_ref[here, head * HD : (head + 1) * HD] = rotated(head)
+        kv_ref[here, :HD] = rotated(heads)
+        kv_ref[here, HD:] = raw[:, (heads + 1) * HD :]
+
+
+def project(blocks, weight, cosine, sine, places):
+    rows = cosine.shape[0]
+    depth, width = weight.shape
+    vmem = pl.BlockSpec(memory_space=pltpu.VMEM)
+    smem = pl.BlockSpec(memory_space=pltpu.SMEM)
+    return pl.pallas_call(
+        functools.partial(project_kernel, len(blocks)),
+        in_specs=[smem] + [vmem] * (len(blocks) + 3),
+        out_specs=[vmem, vmem],
+        out_shape=[
+            jax.ShapeDtypeStruct((rows, width - 2 * HD), BF16),
+            jax.ShapeDtypeStruct((rows, 2 * HD), BF16),
+        ],
+        compiler_params=pltpu.CompilerParams(vmem_limit_bytes=40 * 1024 * 1024),
+        cost_estimate=pl.CostEstimate(
+            flops=2 * rows * depth * width,
+            bytes_accessed=2 * (rows * depth + depth * width),
+            transcendentals=0,
+        ),
+        name="project",
+    )(places, *blocks, weight, cosine, sine)
+
+
+def attend_kernel(q_ref, kv_ref, pos_ref, out_ref):
+    step = pl.program_id(0)
+    size = q_ref.shape[0]
+    span = size + REACH
+    window = pl.ds(pl.multiple_of(step * size, size), span)
+    keys = kv_ref[window, :HD]
+    values = kv_ref[window, HD:]
+    row = lax.broadcasted_iota(jnp.int32, (size, span), 0)
+    column = lax.broadcasted_iota(jnp.int32, (size, span), 1)
+    back = row + REACH - column
+    visible = (back >= 0) & (back <= pos_ref[...])
+    for head in range(q_ref.shape[1] // HD):
+        query = q_ref[:, head * HD : (head + 1) * HD]
+        scores = lax.dot_general(
+            query, keys, (((1,), (1,)), ((), ())), preferred_element_type=F32
+        ) * HD ** (-0.5)
+        scores = jnp.where(visible, scores, -1e30)
+        peak = jnp.max(scores, axis=1, keepdims=True)
+        probs = jnp.exp(scores - peak)
+        total = jnp.sum(probs, axis=1, keepdims=True)
+        mixed = jnp.dot(probs.astype(BF16), values, preferred_element_type=F32)
+        out_ref[:, head * HD : (head + 1) * HD] = (mixed / total).astype(BF16)
+
+
+def attend(queries, keys_values, positions, first, last):
+    size = 256
+    width = queries.shape[1]
+    rows = last - first
+    skip = first // size
+    return pl.pallas_call(
+        attend_kernel,
+        grid=(rows // size,),
+        in_specs=[
+            pl.BlockSpec((size, width), lambda i: (i + skip, 0)),
+            pl.BlockSpec(keys_values.shape, lambda i: (0, 0)),
+            pl.BlockSpec((size, 1), lambda i: (i + skip, 0)),
+        ],
+        out_specs=pl.BlockSpec((size, width), lambda i: (i, 0)),
+        out_shape=jax.ShapeDtypeStruct((rows, width), BF16),
+        compiler_params=pltpu.CompilerParams(vmem_limit_bytes=32 * 1024 * 1024),
+        cost_estimate=pl.CostEstimate(
+            flops=4 * rows * (size + REACH) * width,
+            bytes_accessed=4 * rows * width,
+            transcendentals=rows * (size + REACH) * width // HD,
+        ),
+        name="attend",
+    )(queries, keys_values, positions)
+
+
+def mix_kernel(rows, places, x_ref, w_ref, left_ref, right_ref):
+    half = left_ref.shape[1]
+    for b in range(places.shape[0]):
+        block = x_ref[pl.ds(pl.multiple_of(places[b], 32), rows), :]
+        total = jnp.dot(block, w_ref[...], preferred_element_type=F32).astype(BF16)
+        left_ref[b * rows : (b + 1) * rows, :] = total[:, :half]
+        right_ref[b * rows : (b + 1) * rows, :] = total[:, half:]
+
+
+def mix(attended, weight, places, rows):
+    count = places.shape[0] * rows
+    depth, width = weight.shape
+    vmem = pl.BlockSpec(memory_space=pltpu.VMEM)
+    return pl.pallas_call(
+        functools.partial(mix_kernel, rows),
+        in_specs=[pl.BlockSpec(memory_space=pltpu.SMEM), vmem, vmem],
+        out_specs=[vmem, vmem],
+        out_shape=[jax.ShapeDtypeStruct((count, width // 2), BF16)] * 2,
+        compiler_params=pltpu.CompilerParams(vmem_limit_bytes=40 * 1024 * 1024),
+        cost_estimate=pl.CostEstimate(
+            flops=2 * count * depth * width,
+            bytes_accessed=2 * count * width,
+            transcendentals=0,
+        ),
+        name="mix",
+    )(places, attended, weight)
+
+
+def gate_kernel(blocks, sources, *refs):
+    rows, pieces, out_ref = refs[:blocks], refs[blocks:-1], refs[-1]
+    depth = pieces[0].shape[0]
+    start = 0
+    for block in rows:
+        both = None
+        for k, piece in enumerate(pieces):
+            columns = pl.ds(pl.multiple_of(sources[k] * depth, depth), depth)
+            part = jnp.dot(block[:, columns], piece[...], preferred_element_type=F32)
+            both = part if both is None else both + part
+        half = both.shape[1] // 2
+        gate, up = both[:, :half], both[:, half:]
+        stop = start + block.shape[0]
+        out_ref[start:stop, :] = (gate / (1.0 + jnp.exp(-gate)) * up).astype(BF16)
+        start = stop
+
+
+def gate_up(blocks, pieces, sources):
+    count = sum(block.shape[0] for block in blocks)
+    depth = blocks[0].shape[1]
+    width = pieces[0].shape[1]
+    vmem = pl.BlockSpec(memory_space=pltpu.VMEM)
+    return pl.pallas_call(
+        functools.partial(gate_kernel, len(blocks)),
+        in_specs=[pl.BlockSpec(memory_space=pltpu.SMEM)] + [vmem] * (len(blocks) + len(pieces)),
+        out_specs=vmem,
+        out_shape=jax.ShapeDtypeStruct((count, width // 2), BF16),
+        compiler_params=pltpu.CompilerParams(vmem_limit_bytes=40 * 1024 * 1024),
+        cost_estimate=pl.CostEstimate(
+            flops=2 * count * depth * width,
+            bytes_accessed=2 * (count * depth + depth * width),
+            transcendentals=count * width // 2,
+        ),
+        name="gate_up",
+    )(sources, *blocks, *pieces)
+
+
+def down_kernel(acts_ref, *refs):
+    count = len(refs) // 2
+    for piece, out_ref in zip(refs[:count], refs[count:]):
+        out_ref[...] = jnp.dot(
+            acts_ref[...], piece[...], preferred_element_type=F32
+        ).astype(BF16)
+
+
+def down(acts, pieces):
+    rows, depth = acts.shape
+    width = pieces[0].shape[1]
+    vmem = pl.BlockSpec(memory_space=pltpu.VMEM)
+    return pl.pallas_call(
+        down_kernel,
+        in_specs=[vmem] * (1 + len(pieces)),
+        out_specs=[vmem] * len(pieces),
+        out_shape=[jax.ShapeDtypeStruct((rows, width), BF16)] * len(pieces),
+        compiler_params=pltpu.CompilerParams(vmem_limit_bytes=40 * 1024 * 1024),
+        cost_estimate=pl.CostEstimate(
+            flops=2 * rows * depth * width * len(pieces),
+            bytes_accessed=2 * (rows + depth) * width * len(pieces),
+            transcendentals=0,
+        ),
+        name="down",
+    )(acts, *pieces)
+
+
+def finish_kernel(count, sources, pair_sources, mixed_ref, *refs):
+    own, pair, (out_ref, total) = refs[:count], refs[count:-2], refs[-2:]
+    width = own[0].shape[1]
+
+    def at(place):
+        return pl.ds(pl.multiple_of(place * width, width), width)
+
+    for k in range(count):
+        columns = at(sources[k])
+        total[:, columns] = mixed_ref[:, columns] + own[k][...]
+    for k in range(count):
+        columns = at(pair_sources[k])
+        out_ref[:, columns] = (total[:, columns] + pair[k][...].astype(F32)).astype(BF16)
+
+
+def finish(mixed, own, pair, sources, pair_sources):
+    vmem = pl.BlockSpec(memory_space=pltpu.VMEM)
+    smem = pl.BlockSpec(memory_space=pltpu.SMEM)
+    return pl.pallas_call(
+        functools.partial(finish_kernel, len(own)),
+        in_specs=[smem, smem] + [vmem] * (1 + 2 * len(own)),
+        out_specs=vmem,
+        out_shape=jax.ShapeDtypeStruct(mixed.shape, BF16),
+        scratch_shapes=[pltpu.VMEM(mixed.shape, F32)],
+        compiler_params=pltpu.CompilerParams(vmem_limit_bytes=16 * 1024 * 1024),
+        name="finish",
+    )(sources, pair_sources, mixed, *own, *pair)
+
+
+def body(
+    hidden,
+    request_of,
+    positions,
+    page_table,
+    attn_gain,
+    mlp_gain,
+    wq,
+    wk,
+    wv,
+    wo,
+    w_gate,
+    w_up,
+    w_down,
+):
+    groups = lax.axis_size("group")
+    me = lax.axis_index("tensor")
+    group = lax.axis_index("group")
+    odd = group % 2 == 1
+    tok_group = request_of.shape[0]
+    depth = hidden.shape[1]
+    rows_dev = hidden.shape[0]
+    sources = jnp.stack([(group - k) % groups for k in range(groups)]).astype(jnp.int32)
+    pair_sources = jnp.stack([((group ^ 1) - k) % groups for k in range(groups)]).astype(jnp.int32)
+    starts = []
+    for k in ORDER:
+        first = (me ^ k) * rows_dev
+        starts += [first, first + rows_dev // 2] if k in (6, 7) else [first]
+    places = jnp.stack(starts).astype(jnp.int32)
+
+    small = jnp.concatenate([wq.astype(BF16), wk.astype(BF16), wv.astype(BF16)], axis=1)
+    qkv_weight = lax.all_gather(small, "group", axis=0, tiled=True)
+    own_normed = rms_scale(hidden.astype(F32), attn_gain)
+    firsts = gather_first(own_normed)
+    far = gather_far(firsts)
+    near = near_blocks(own_normed, firsts, far)
+    normed = near + over(near)
+    out_weight = lax.all_gather(wo.astype(BF16), "group", axis=1, tiled=True)
+
+    half_dim = HD // 2
+    frequency = rope_base ** (-(jnp.arange(half_dim, dtype=F32) * 2.0 / HD))
+    angle = positions.astype(F32)[:, None] * frequency[None, :]
+    cosine, sine = jnp.cos(angle), jnp.sin(angle)
+    cosine = jnp.concatenate([cosine, cosine], axis=1)
+    sine = jnp.concatenate([-sine, sine], axis=1)
+
+    queries, kv_rows = project(normed, qkv_weight, cosine, sine, places)
+    earlier = from_behind(kv_rows[-REACH:])
+    places_in = positions[:, None]
+    late = attend(queries, kv_rows, places_in, REACH, tok_group)
+    early_kv = jnp.concatenate([earlier, kv_rows[:REACH]], axis=0)
+    early = attend(queries, early_kv, places_in, 0, REACH)
+    attended = jnp.concatenate([early, late], axis=0)
+
+    ff = w_gate.shape[1] // 2
+    gate_b, up_b, down_b = w_gate.astype(BF16), w_up.astype(BF16), w_down.astype(BF16)
+    lower = jnp.concatenate([gate_b[:, :ff], up_b[:, :ff]], axis=1)
+    upper = jnp.concatenate([gate_b[:, ff:], up_b[:, ff:]], axis=1)
+    mine_in = jnp.where(odd, upper, lower)
+    other_in = jnp.where(odd, lower, upper)
+    mine_out = jnp.where(odd, down_b[ff:], down_b[:ff])
+    other_out = jnp.where(odd, down_b[:ff], down_b[ff:])
+    gated_in = after(other_in, late)
+    in_pieces = [mine_in] + [None] * (groups - 1)
+    for distance in range(1, groups, 2):
+        in_pieces[distance] = turn(gated_in, distance)
+
+    pages = page_table.shape[1]
+    changed = jnp.concatenate(
+        [jnp.ones((1,), jnp.int32), (request_of[1:] != request_of[:-1]).astype(jnp.int32)]
+    )
+    opens = jnp.maximum(changed, (positions % PAGE == 0).astype(jnp.int32))
+    logical = jnp.cumsum(opens) - 1
+    chosen = jnp.sum(
+        jnp.where(logical[:, None] == jnp.arange(pages)[None, :], page_table, 0), axis=1
+    )
+    target = chosen * PAGE + positions % PAGE
+    width = kv_rows.shape[1]
+    cache = jnp.zeros((pages * PAGE, width), BF16).at[target].set(kv_rows)
+
+    four = len(ORDER) // 2
+    block_places = jnp.stack([(me ^ k) * rows_dev for k in ORDER]).astype(jnp.int32)
+    other = mix(attended, out_weight, block_places[four:], rows_dev)
+    mine = mix(attended, out_weight, block_places[:four], rows_dev)
+    sums = jnp.concatenate(scatter_sum(mine, other), axis=1)
+    sums, in_pieces[1] = tied(sums, in_pieces[1])
+    mixed = hidden.astype(F32) + sums
+    normed_mlp = rms_scale(mixed, mlp_gain)
+
+    other_rows = pair_swap(normed_mlp)
+    firsts = gather_first(normed_mlp)
+    firsts, cache, in_pieces[3], mine_in = tied(firsts, cache, in_pieces[3], mine_in)
+    in_pieces[2] = turn(mine_in, 2)
+    own_near = near_blocks(normed_mlp, firsts, gather_far(firsts))
+    own_blocks = [own_near, over(own_near)]
+    other_rows = after(other_rows, own_near)
+    firsts = gather_first(other_rows)
+    firsts, in_pieces[2], mine_out, other_out = tied(firsts, in_pieces[2], mine_out, other_out)
+    other_near = near_blocks(other_rows, firsts, gather_far(firsts))
+    other_blocks = [other_near, over(other_near)]
+    out_pieces = [mine_out]
+    for distance in range(1, groups):
+        out_pieces.append(turn(mine_out if distance % 2 == 0 else other_out, distance))
+
+    def acts_of(blocks):
+        near, across = blocks
+        return gate_up(across, in_pieces, sources), gate_up(near, in_pieces, sources)
+
+    def sums_of(acts, pieces):
+        across, near = acts
+        other = down(across, pieces)
+        return scatter_sum(down(near, pieces), other)
+
+    own_acts = acts_of(own_blocks)
+    other_acts = acts_of(other_blocks)
+    order, own_sums, pair_sums = [], [], []
+    for first, second in ((0, 1), (3, 2)):
+        pieces = [out_pieces[first], out_pieces[second]]
+        order += [first, second]
+        pair = jnp.concatenate([half.astype(BF16) for half in sums_of(other_acts, pieces)], axis=1)
+        own_sums += sums_of(own_acts, pieces)
+        pair = pair_swap(pair)
+        pair_sums += [pair[:, : pair.shape[1] // 2], pair[:, pair.shape[1] // 2 :]]
+    order = jnp.array(order)
+    layer_out = finish(mixed, own_sums, pair_sums, sources[order], pair_sources[order])
+    return (layer_out, cache.reshape(pages, PAGE, width))
 
 
 def partner(value, axis, distance):
@@ -19,13 +445,13 @@
     return lax.ppermute(value, axis, pairs)
 
 
-def from_behind(block, axis, distance):
+def plain_from_behind(block, axis, distance):
     devices = range(lax.axis_size(axis))
     route = [(i - distance, i) for i in devices if i - distance in devices]
     return lax.ppermute(block, axis, route)
 
 
-def rms_scale(values, gain):
+def plain_rms_scale(values, gain):
     square = jnp.mean(values * values, axis=-1, keepdims=True)
     return (values * lax.rsqrt(square + norm_eps) * gain).astype(jnp.bfloat16)
 
@@ -55,7 +481,7 @@
     return tuple((jnp.dot(acts, piece, preferred_element_type=jnp.float32) for piece in pieces))
 
 
-def body(
+def plain_body(
     hidden,
     request_of,
     positions,
@@ -78,7 +504,7 @@
     group_ratio = QH // KVH
     paired = tensor_count > KVH
     residual = lax.all_gather(hidden, "tensor", axis=0, tiled=True).astype(jnp.float32)
-    normed = rms_scale(residual, attn_gain)
+    normed = plain_rms_scale(residual, attn_gain)
     query_rows = wq.astype(jnp.bfloat16)
     key_rows = wk.astype(jnp.bfloat16)
     value_rows = wv.astype(jnp.bfloat16)
@@ -101,7 +527,7 @@
     keys = rotate(key_raw.reshape(tok_group, key_heads, HD), positions)
     values = value_raw.reshape(tok_group, key_heads, HD)
     kv_rows = jnp.stack([keys, values], axis=2)
-    earlier = from_behind(kv_rows, "group", 1)
+    earlier = plain_from_behind(kv_rows, "group", 1)
     earlier_rows = earlier.shape[0]
     all_rows = jnp.concatenate([earlier, kv_rows], axis=0)
     all_keys = jnp.repeat(all_rows[:, :, 0], group_ratio, axis=1)[:, :query_heads]
@@ -133,7 +559,7 @@
         preferred_element_type=jnp.float32,
     )
     mixed = residual + lax.psum(attn_part.astype(jnp.bfloat16), "tensor").astype(jnp.float32)
-    normed_mlp = rms_scale(mixed, mlp_gain)
+    normed_mlp = plain_rms_scale(mixed, mlp_gain)
     gate_rows = w_gate.astype(jnp.bfloat16)
     up_rows = w_up.astype(jnp.bfloat16)
     gate_sum, up_sum = contract_rows(
@@ -174,6 +600,7 @@
 
 
 def solution(mesh):
+    shaped = mesh.shape["tensor"] == len(ORDER) and mesh.shape["group"] == 4
     placed = (
         P(("group", "tensor"), None),
         P("group"),
@@ -190,7 +617,7 @@
         P("tensor", "group"),
     )
     return jax.shard_map(
-        body,
+        body if shaped else plain_body,
         mesh=mesh,
         in_specs=placed,
         out_specs=(P(("group", "tensor"), None), P("group", None, "tensor")),

time: 649 us -> 402 us (0.62)
  waiting for transfers between devices: 422 us -> 180 us
  matrix products: 94.7 us -> 0 us
  starting transfers between devices: 4.03 us -> 78.6 us
  Pallas kernels: 0 us -> 50.1 us
  blocking collectives: 34.3 us -> 0 us
  local copies, waits for them, and re-layouts: 18.9 us -> 41.6 us
  other arithmetic: 52.1 us -> 32.8 us
    all_gather x6 -> x2, waiting for transfers between devices: 230 us -> 14.9 us  [the longest x1 7.87 us: body(): qkv_weight = lax.all_gather(small, 'group', axis=0, tiled=True)]
    psum x2 -> x0, waiting for transfers between devices: 191 us -> none  [the longest x1 99.8 us: body(): lax.psum(attn_part.astype(jnp.bfloat16), 'tensor').astype(jnp.float32)]
    ppermute x1 -> x67, waiting for transfers between devices: 0.01 us -> 165 us  [the longest x57 82.3 us: swap(): lax.ppermute(value, 'tensor', [(i, i ^ distance) for i in range(lax.axis_...]
    ppermute x1 -> x67, starting transfers between devices: 3.7 us -> 78.5 us  [the longest x57 46.9 us: swap(): lax.ppermute(value, 'tensor', [(i, i ^ distance) for i in range(lax.axis_...]
    dot_general x7 -> x0, matrix products: 72.6 us -> none  [the longest x1 22.6 us: body(): jnp.dot(activation, lax.all_gather(down_rows, 'group', axis=1, tiled=True...]
    pallas_call x0 -> x18, Pallas kernels: none -> 50.1 us  [the longest x4 24.2 us: gate_up(): pl.pallas_call(functools.partial(gate_kernel, len(blocks)), in_specs=[pl....]
    all_gather x2 -> x0, blocking collectives: 34.3 us -> none  [the longest x1 17.4 us: body(): lax.all_gather(key_rows, 'group', axis=0, tiled=True)]
    sub x1 -> x0, matrix products: 22 us -> none  [body(): probs = jnp.where(visible[None], jnp.exp(scores - row_peak), 0.0)]
  transfers between devices with their start and end apart: 9 -> 69, of which waited for: 6 -> 25; matrix products, arithmetic and copies ran while one was open for 21% -> 15% of each run, Pallas kernels for 0% -> 12%
where the time goes in v2:
time: 402 us; the launch traced here: 398 us
  waiting for transfers between devices  180 us (45%)
  starting transfers between devices  78.6 us (20%)
  Pallas kernels  50.1 us (12%)
  local copies, waits for them, and re-layouts  41.6 us (10%)
  other arithmetic  32.8 us (8%)
  between operations  15.2 us (4%)
    ppermute x57, waiting for transfers between devices, swap(): lax.ppermute(value, 'tensor', [(i, i ^ distance) for i in range(lax.axis_...  82.3 us
    ppermute x6, waiting for transfers between devices, turn(): lax.ppermute(value, 'group', [(i, (i + distance) % count) for i in range(...  65.9 us
    ppermute x57, starting transfers between devices, swap(): lax.ppermute(value, 'tensor', [(i, i ^ distance) for i in range(lax.axis_...  46.9 us
    ppermute x6, starting transfers between devices, turn(): lax.ppermute(value, 'group', [(i, (i + distance) % count) for i in range(...  28.9 us
    pallas_call x4, Pallas kernels, gate_up(): pl.pallas_call(functools.partial(gate_kernel, len(blocks)), in_specs=[pl....  24.2 us
    scatter x1, local copies, waits for them, and re-layouts, body(): cache = jnp.zeros((pages * PAGE, width), BF16).at[target].set(kv_rows)  22.8 us
    ppermute x3, waiting for transfers between devices, pair_swap(): lax.ppermute(value, 'group', [(i, i ^ 1) for i in range(lax.axis_size('gr...  10.5 us
    unnamed x58, local copies, waits for them, and re-layouts  9.99 us
  transfers between devices with their start and end apart: 69, of which 25 were waited for; matrix products, arithmetic and copies ran while one was open for 15% of the time, Pallas kernels for 12%

profile of v2, /device:TPU:0, one launch (start us, length us, event | category | flops | bytes accessed | tf_op | source)
XLA Modules:
  0.0 398.2 jit_solution(15127431224928467728)
XLA Ops:
  11.8 3.0 collective-permute-start
  14.8 1.5 collective-permute-start.2
  17.9 14.5 %collective-permute-done.refs_0_ = bf16[192,2048]{1,0:T(8,128)(2,1)S(1)} collective-permute-done((bf16[192,2048]{1,0:T(8,128)(2,1)S(1)}, bf16[192,2048]{1,0:T(8,128)(2,1)S(1)}, u32[]{:S(2)}, u32[]{:S(2)}) %collective-permute-start) | collective-permute-done | bytes 786464 | tf_op jit(solution)/shard_map/ppermute | solution.py:26
  32.4 1.8 collective-permute-start.1
  35.2 1.6 collective-permute-start.3
  38.1 4.8 %collective-permute-done.1.refs_1_ = bf16[96,2048]{1,0:T(8,128)(2,1)S(1)} collective-permute-done((bf16[96,2048]{1,0:T(8,128)(2,1)S(1)}, bf16[96,2048]{1,0:T(8,128)(2,1)S(1)}, u32[]{:S(2)}, u32[]{:S(2)}) %collective-permute-start.1) | collective-permute-done | bytes 393248 | tf_op jit(solution)/shard_map/ppermute | solution.py:26
  42.9 2.4 collective-permute-done.3.refs_2_
  45.2 4.4 %fusion.5 = (f32[1536,64]{1,0:T(8,128)}, f32[1536,64]{1,0:T(8,128)}, f32[1536,64]{1,0:T(8,128)}) fusion(f32[64]{0:T(128)S(1)} %negate_power_fusion, f32[1536]{0:T(1024)S(1)} %get-tuple-element.94), kind=kLoop, calls=%fused_computation.61 | loop fusion | flops 196608 | bytes 1186048 | tf_op jit(solution)/shard_map/neg | solution.py:358
  49.7 2.3 pad_maximum_fusion.3
  52.1 7.9 %all-gather.3.cloned.1.call-done.refs_10_ = bf16[2048,512]{1,0:T(8,128)(2,1)} async-done(((bf16[512,512]{1,0:T(8,128)(2,1)}), bf16[2048,512]{1,0:T(8,128)(2,1)}) %all-gather.3.cloned.1.call-update) | async-done | bytes 2097168 | tf_op jit(solution)/shard_map/all_gather | solution.py:345
  60.0 1.6 copy-done.5
  61.6 6.3 %project.1 = (bf16[1536,256]{1,0:T(8,128)(2,1)S(1)}, bf16[1536,256]{1,0:T(8,128)(2,1)S(1)}) custom-call(s32[10]{0:T(128)S(1)} %stack.97.places, bf16[192,2048]{1,0:T(8,128)(2,1)S(1)} %collective-permute-done.refs_0_, bf16[96,2048]{1,0:T(8,128)(2,1)S(1)} %collective-permute-done.1.refs_1_, bf16[96,2048]{1,0:T(8,128)(2,1)} %collective-permute-done.3.refs_2_, ...), custom_call_target="tpu_custom_call" | custom-call | flops 3221225472 | bytes 8388608 | tf_op jit(solution)/shard_map/project/pallas_call | solution.py:126
  67.9 2.2 collective-permute-start.9
  70.4 4.7 %attend.3 = bf16[1024,256]{1,0:T(8,128)(2,1)S(1)} custom-call(bf16[1536,256]{1,0:T(8,128)(2,1)S(1)} %get-tuple-element.38.q_ref, bf16[1536,256]{1,0:T(8,128)(2,1)S(1)} %get-tuple-element.39.kv_ref, s32[1536,1]{1,0:T(8,128)S(1)} %broadcast_in_dim.42.pos_ref), custom_call_target="tpu_custom_call" | custom-call | flops 805306368 | bytes 1048576 | tf_op jit(solution)/shard_map/attend/pallas_call | solution.py:173
  75.1 6.3 %collective-permute-done.9 = bf16[512,256]{1,0:T(8,128)(2,1)S(1)} collective-permute-done((bf16[512,256]{1,0:T(8,128)(2,1)S(1)}, bf16[512,256]{1,0:T(8,128)(2,1)S(1)}, u32[]{:S(2)}, u32[]{:S(2)}) %collective-permute-start.9) | collective-permute-done | bytes 262176 | tf_op jit(solution)/shard_map/ppermute | solution.py:42
  81.5 2.3 attend.2
  83.9 7.0 %all-gather.5.cloned.1.call-done.w_ref = bf16[256,2048]{1,0:T(8,128)(2,1)} async-done(((bf16[256,512]{1,0:T(8,128)(2,1)}), bf16[256,2048]{1,0:T(8,128)(2,1)}) %all-gather.5.cloned.1.call-update) | async-done | bytes 1048592 | tf_op jit(solution)/shard_map/all_gather | solution.py:351
  92.2 1.5 mix.3
  95.5 1.5 mix.2
  97.2 1.4 add_convert_fusion
  98.6 2.2 collective-permute-start.14
  103.1 1.5 collective-permute-start.11
  104.6 1.9 convert_element_type.409
  107.2 11.7 %collective-permute-done.14 = bf16[384,1024]{1,0:T(8,128)(2,1)} collective-permute-done((bf16[384,1024]{1,0:T(8,128)(2,1)}, bf16[384,1024]{1,0:T(8,128)(2,1)}, u32[]{:S(2)}, u32[]{:S(2)}) %collective-permute-start.14) | collective-permute-done | bytes 786464 | tf_op jit(solution)/shard_map/ppermute | solution.py:26
  120.1 1.8 collective-permute-start.15
  121.9 1.9 broadcast_select_fusion
  123.8 2.3 collective-permute-start.16
  127.3 1.5 collective-permute-start.12
  128.8 1.9 collective-permute-start.19
  132.3 4.8 %collective-permute-done.12 = bf16[192,1024]{1,0:T(8,128)(2,1)S(1)} collective-permute-done((bf16[192,1024]{1,0:T(8,128)(2,1)S(1)}, bf16[192,1024]{1,0:T(8,128)(2,1)S(1)}, u32[]{:S(2)}, u32[]{:S(2)}) %collective-permute-start.12) | collective-permute-done | bytes 393248 | tf_op jit(solution)/shard_map/ppermute | solution.py:26
  137.1 1.2 convert_add_fusion.2
  138.5 13.7 %collective-permute-done.16.refs_6_ = bf16[512,1024]{1,0:T(8,128)(2,1)S(1)} collective-permute-done((bf16[512,1024]{1,0:T(8,128)(2,1)}, bf16[512,1024]{1,0:T(8,128)(2,1)S(1)}, u32[]{:S(2)}, u32[]{:S(2)}) %collective-permute-start.16) | collective-permute-done | bytes 1048608 | tf_op jit(solution)/shard_map/ppermute | solution.py:33
  154.4 1.5 collective-permute-start.18
  156.0 22.8 %scatter_custom_fusion = bf16[8192,256]{1,0:T(8,128)(2,1)} fusion(s32[1536]{0:T(1024)} %get-tuple-element.93, bf16[1536,256]{1,0:T(8,128)(2,1)} %copy-done.4, bf16[]{:T(256)} %constant.126.clone.1), kind=kCustom, calls=%fused_computation.6 | custom fusion | bytes 4194816 | tf_op jit(solution)/shard_map/scatter | solution.py:392
  181.5 1.6 collective-permute-start.21
  183.1 20.9 %collective-permute-start.25 = (bf16[512,1024]{1,0:T(8,128)(2,1)S(1)}, bf16[512,1024]{1,0:T(8,128)(2,1)S(1)}, u32[]{:S(2)}, u32[]{:S(2)}) collective-permute-start(bf16[512,1024]{1,0:T(8,128)(2,1)S(1)} %copy-done), channel_id=1, source_target_pairs={{0,16},{8,24},{16,0},{24,8},{1,17},{9,25},{17,1},{25,9},{2,18},{10... | collective-permute-start | bytes 3145736 | tf_op jit(solution)/shard_map/ppermute | solution.py:33
  205.7 21.7 %collective-permute-done.25.refs_7_ = bf16[512,1024]{1,0:T(8,128)(2,1)S(1)} collective-permute-done((bf16[512,1024]{1,0:T(8,128)(2,1)S(1)}, bf16[512,1024]{1,0:T(8,128)(2,1)S(1)}, u32[]{:S(2)}, u32[]{:S(2)}) %collective-permute-start.25) | collective-permute-done | bytes 1048608 | tf_op jit(solution)/shard_map/ppermute | solution.py:33
  228.5 2.7 convert_element_type.413
  232.6 2.2 broadcast_select_fusion.2
  234.8 1.8 slice.377
  236.6 1.8 slice.378
  243.6 6.1 %gate_up.4.acts_ref = bf16[768,512]{1,0:T(8,128)(2,1)S(1)} custom-call(s32[4]{0:T(128)S(1)} %pad_add_fusion.sources, bf16[192,2048]{1,0:T(8,128)(2,1)} %collective-permute-done.17.refs_0_, bf16[96,2048]{1,0:T(8,128)(2,1)} %collective-permute-done.20.refs_1_, bf16[96,2048]{1,0:T(8,128)(2,1)} %collective-permute-done.21.refs_2_, ...), custom_call_target="tpu_custom_call" | custom-call | flops 3221225472 | bytes 7340032 | tf_op jit(solution)/shard_map/gate_up/pallas_call | solution.py:243
  249.8 3.8 collective-permute-start.38
  254.1 6.2 %gate_up.5.acts_ref = bf16[768,512]{1,0:T(8,128)(2,1)S(1)} custom-call(s32[4]{0:T(128)S(1)} %pad_add_fusion.sources, bf16[192,2048]{1,0:T(8,128)(2,1)} %collective-permute-done.27.refs_0_, bf16[96,2048]{1,0:T(8,128)(2,1)} %collective-permute-done.28.refs_1_, bf16[96,2048]{1,0:T(8,128)(2,1)} %collective-permute-done.29.refs_2_, ...), custom_call_target="tpu_custom_call" | custom-call | flops 3221225472 | bytes 7340032 | tf_op jit(solution)/shard_map/gate_up/pallas_call | solution.py:243
  260.3 6.2 %gate_up.6.acts_ref = bf16[768,512]{1,0:T(8,128)(2,1)S(1)} custom-call(s32[4]{0:T(128)S(1)} %pad_add_fusion.sources, bf16[192,2048]{1,0:T(8,128)(2,1)} %collective-permute-done.23.refs_0_, bf16[96,2048]{1,0:T(8,128)(2,1)} %collective-permute-done.46.refs_1_, bf16[96,2048]{1,0:T(8,128)(2,1)} %collective-permute-done.47.refs_2_, ...), custom_call_target="tpu_custom_call" | custom-call | flops 3221225472 | bytes 7340032 | tf_op jit(solution)/shard_map/gate_up/pallas_call | solution.py:243
  266.7 7.7 %collective-permute-done.38.refs_0_ = bf16[512,512]{1,0:T(8,128)(2,1)S(1)} collective-permute-done((bf16[512,512]{1,0:T(8,128)(2,1)S(1)}, bf16[512,512]{1,0:T(8,128)(2,1)S(1)}, u32[]{:S(2)}, u32[]{:S(2)}) %collective-permute-start.38) | collective-permute-done | bytes 524320 | tf_op jit(solution)/shard_map/ppermute | solution.py:33
  275.4 22.7 %collective-permute-done.39.refs_1_ = bf16[512,512]{1,0:T(8,128)(2,1)S(1)} collective-permute-done((bf16[512,512]{1,0:T(8,128)(2,1)S(1)}, bf16[512,512]{1,0:T(8,128)(2,1)S(1)}, u32[]{:S(2)}, u32[]{:S(2)}) %collective-permute-start.39) | collective-permute-done | bytes 524320 | tf_op jit(solution)/shard_map/ppermute | solution.py:33
  304.2 5.7 %gate_up.7.acts_ref = bf16[768,512]{1,0:T(8,128)(2,1)S(1)} custom-call(s32[4]{0:T(128)S(1)} %pad_add_fusion.sources, bf16[192,2048]{1,0:T(8,128)(2,1)S(1)} %collective-permute-done.48.refs_0_, bf16[96,2048]{1,0:T(8,128)(2,1)S(1)} %collective-permute-done.49.refs_1_, bf16[96,2048]{1,0:T(8,128)(2,1)S(1)} %collective-permute-done.50.refs_2_, ...), custom_call_target="tpu_custom_call" | custom-call | flops 3221225472 | bytes 7340032 | tf_op jit(solution)/shard_map/gate_up/pallas_call | solution.py:243
  314.6 1.7 collective-permute-start.36
  318.2 1.7 collective-permute-start.57
  320.0 5.5 %collective-permute-done.33 = bf16[384,512]{1,0:T(8,128)(2,1)S(1)} collective-permute-done((bf16[384,512]{1,0:T(8,128)(2,1)S(1)}, bf16[384,512]{1,0:T(8,128)(2,1)S(1)}, u32[]{:S(2)}, u32[]{:S(2)}) %collective-permute-start.33) | collective-permute-done | bytes 393248 | tf_op jit(solution)/shard_map/ppermute | solution.py:26
  326.6 1.7 collective-permute-start.64
  328.4 5.6 %collective-permute-done.41 = bf16[384,512]{1,0:T(8,128)(2,1)S(1)} collective-permute-done((bf16[384,512]{1,0:T(8,128)(2,1)S(1)}, bf16[384,512]{1,0:T(8,128)(2,1)S(1)}, u32[]{:S(2)}, u32[]{:S(2)}) %collective-permute-start.41) | collective-permute-done | bytes 393248 | tf_op jit(solution)/shard_map/ppermute | solution.py:26
  335.1 1.7 collective-permute-start.34
  336.8 18.2 %collective-permute-done.34 = bf16[192,512]{1,0:T(8,128)(2,1)S(1)} collective-permute-done((bf16[192,512]{1,0:T(8,128)(2,1)S(1)}, bf16[192,512]{1,0:T(8,128)(2,1)S(1)}, u32[]{:S(2)}, u32[]{:S(2)}) %collective-permute-start.34) | collective-permute-done | bytes 196640 | tf_op jit(solution)/shard_map/ppermute | solution.py:26
  356.2 4.5 %collective-permute-done.37 = bf16[192,512]{1,0:T(8,128)(2,1)S(1)} collective-permute-done((bf16[192,512]{1,0:T(8,128)(2,1)S(1)}, bf16[192,512]{1,0:T(8,128)(2,1)S(1)}, u32[]{:S(2)}, u32[]{:S(2)}) %collective-permute-start.37) | collective-permute-done | bytes 196640 | tf_op jit(solution)/shard_map/ppermute | solution.py:26
  360.7 1.7 collective-permute-start.42
  362.4 3.9 collective-permute-done.42
  368.7 1.7 collective-permute-start.55
  372.2 3.8 collective-permute-done.58
  376.4 1.8 collective-permute-done.65
  378.9 6.3 %collective-permute-done.59 = bf16[192,1024]{1,0:T(8,128)(2,1)S(1)} collective-permute-done((bf16[192,1024]{1,0:T(8,128)(2,1)S(1)}, bf16[192,1024]{1,0:T(8,128)(2,1)S(1)}, u32[]{:S(2)}, u32[]{:S(2)}) %collective-permute-start.59) | collective-permute-done | bytes 393248 | tf_op jit(solution)/shard_map/ppermute | solution.py:37
  385.2 4.2 %collective-permute-done.66 = bf16[192,1024]{1,0:T(8,128)(2,1)S(1)} collective-permute-done((bf16[192,1024]{1,0:T(8,128)(2,1)S(1)}, bf16[192,1024]{1,0:T(8,128)(2,1)S(1)}, u32[]{:S(2)}, u32[]{:S(2)}) %collective-permute-start.66) | collective-permute-done | bytes 393248 | tf_op jit(solution)/shard_map/ppermute | solution.py:37
  389.4 1.8 finish.1
  (235 shorter events, 56.6 us)
Async XLA Ops:
  7.2 52.8 %all-gather.3.cloned.1.call-start = ((), (), s32[]{:S(2)}) async-start(), calls=%async_computation | async-start | bytes 2621440 | tf_op jit(solution)/shard_map/all_gather | solution.py:345
  11.2 79.7 %all-gather.5.cloned.1.call-start = ((), (), s32[]{:S(2)}) async-start(), calls=%async_computation.1 | async-start | bytes 1310720 | tf_op jit(solution)/shard_map/all_gather | solution.py:351
  11.8 20.5 %collective-permute-start = (bf16[192,2048]{1,0:T(8,128)(2,1)S(1)}, bf16[192,2048]{1,0:T(8,128)(2,1)S(1)}, u32[]{:S(2)}, u32[]{:S(2)}) collective-permute-start(bf16[192,2048]{1,0:T(8,128)(2,1)S(1)} %fusion.4.refs_4_), channel_id=1, source_target_pairs={{0,2},{1,3},{2,0},{3,1},{4,6},{5,7},{6,4},{7,5},{8,10},{9,11},{10,... | collective-permute-start | bytes 2359304 | tf_op jit(solution)/shard_map/ppermute | solution.py:26
  14.8 19.4 %collective-permute-start.2 = (bf16[192,2048]{1,0:T(8,128)(2,1)S(1)}, bf16[192,2048]{1,0:T(8,128)(2,1)}, u32[]{:S(2)}, u32[]{:S(2)}) collective-permute-start(bf16[192,2048]{1,0:T(8,128)(2,1)S(1)} %fusion.4.refs_4_), channel_id=1, source_target_pairs={{0,4},{1,5},{2,6},{3,7},{4,0},{5,1},{6,2},{7,3},{8,12},{9,13},{10,... | collective-permute-start | bytes 2359304 | tf_op jit(solution)/shard_map/ppermute | solution.py:26
  16.3 35.7 %collective-permute-start.8 = (bf16[192,2048]{1,0:T(8,128)(2,1)S(1)}, bf16[192,2048]{1,0:T(8,128)(2,1)}, u32[]{:S(2)}, u32[]{:S(2)}) collective-permute-start(bf16[192,2048]{1,0:T(8,128)(2,1)S(1)} %fusion.4.refs_4_), channel_id=1, source_target_pairs={{0,1},{1,0},{2,3},{3,2},{4,5},{5,4},{6,7},{7,6},{8,9},{9,8},{10,11... | collective-permute-start | bytes 2359304 | tf_op jit(solution)/shard_map/ppermute | solution.py:26
  32.4 10.5 %collective-permute-start.1 = (bf16[96,2048]{1,0:T(8,128)(2,1)S(1)}, bf16[96,2048]{1,0:T(8,128)(2,1)S(1)}, u32[]{:S(2)}, u32[]{:S(2)}) collective-permute-start(bf16[96,2048]{1,0:T(8,128)(2,1)S(1)} %slice.419), channel_id=1, source_target_pairs={{0,4},{1,5},{2,6},{3,7},{4,0},{5,1},{6,2},{7,3},{8,12},{9,13},{10,... | collective-permute-start | bytes 1179656 | tf_op jit(solution)/shard_map/ppermute | solution.py:26
  35.2 10.0 %collective-permute-start.3 = (bf16[96,2048]{1,0:T(8,128)(2,1)S(1)}, bf16[96,2048]{1,0:T(8,128)(2,1)}, u32[]{:S(2)}, u32[]{:S(2)}) collective-permute-start(bf16[96,2048]{1,0:T(8,128)(2,1)S(1)} %slice.420), channel_id=1, source_target_pairs={{0,2},{1,3},{2,0},{3,1},{4,6},{5,7},{6,4},{7,5},{8,10},{9,11},{10,... | collective-permute-start | bytes 1179656 | tf_op jit(solution)/shard_map/ppermute | solution.py:26
  37.6 14.5 %collective-permute-start.4 = (bf16[192,2048]{1,0:T(8,128)(2,1)S(1)}, bf16[192,2048]{1,0:T(8,128)(2,1)}, u32[]{:S(2)}, u32[]{:S(2)}) collective-permute-start(bf16[192,2048]{1,0:T(8,128)(2,1)S(1)} %collective-permute-done.refs_0_), channel_id=1, source_target_pairs={{0,1},{1,0},{2,3},{3,2},{4,5},{5,4},{6,7},{7,6},{8,9},{9,8},{10,11... | collective-permute-start | bytes 2359304 | tf_op jit(solution)/shard_map/ppermute | solution.py:26
  37.6 14.5 %collective-permute-start.7 = (bf16[192,2048]{1,0:T(8,128)(2,1)}, bf16[192,2048]{1,0:T(8,128)(2,1)}, u32[]{:S(2)}, u32[]{:S(2)}) collective-permute-start(bf16[192,2048]{1,0:T(8,128)(2,1)} %collective-permute-done.2.refs_3_), channel_id=1, source_target_pairs={{0,1},{1,0},{2,3},{3,2},{4,5},{5,4},{6,7},{7,6},{8,9},{9,8},{10,11... | collective-permute-start | bytes 2359304 | tf_op jit(solution)/shard_map/ppermute | solution.py:26
  42.9 9.2 %collective-permute-start.5 = (bf16[96,2048]{1,0:T(8,128)(2,1)S(1)}, bf16[96,2048]{1,0:T(8,128)(2,1)}, u32[]{:S(2)}, u32[]{:S(2)}) collective-permute-start(bf16[96,2048]{1,0:T(8,128)(2,1)S(1)} %collective-permute-done.1.refs_1_), channel_id=1, source_target_pairs={{0,1},{1,0},{2,3},{3,2},{4,5},{5,4},{6,7},{7,6},{8,9},{9,8},{10,11... | collective-permute-start | bytes 1179656 | tf_op jit(solution)/shard_map/ppermute | solution.py:26
  45.2 6.9 %collective-permute-start.6 = (bf16[96,2048]{1,0:T(8,128)(2,1)}, bf16[96,2048]{1,0:T(8,128)(2,1)}, u32[]{:S(2)}, u32[]{:S(2)}) collective-permute-start(bf16[96,2048]{1,0:T(8,128)(2,1)} %collective-permute-done.3.refs_2_), channel_id=1, source_target_pairs={{0,1},{1,0},{2,3},{3,2},{4,5},{5,4},{6,7},{7,6},{8,9},{9,8},{10,11... | collective-permute-start | bytes 1179656 | tf_op jit(solution)/shard_map/ppermute | solution.py:26
  67.9 13.5 %collective-permute-start.9 = (bf16[512,256]{1,0:T(8,128)(2,1)S(1)}, bf16[512,256]{1,0:T(8,128)(2,1)S(1)}, u32[]{:S(2)}, u32[]{:S(2)}) collective-permute-start(bf16[512,256]{1,0:T(8,128)(2,1)S(1)} %get-tuple-element.84), channel_id=1, source_target_pairs={{0,8},{8,16},{16,24},{1,9},{9,17},{17,25},{2,10},{10,18},{18,26},{... | collective-permute-start | bytes 786440 | tf_op jit(solution)/shard_map/ppermute | solution.py:42
  93.8 6.9 %collective-permute-start.10 = (bf16[768,1024]{1,0:T(8,128)(2,1)S(1)}, bf16[768,1024]{1,0:T(8,128)(2,1)S(1)}, u32[]{:S(2)}, u32[]{:S(2)}) collective-permute-start(bf16[768,1024]{1,0:T(8,128)(2,1)S(1)} %get-tuple-element.41), channel_id=1, source_target_pairs={{0,1},{1,0},{2,3},{3,2},{4,5},{5,4},{6,7},{7,6},{8,9},{9,8},{10,11... | collective-permute-start | bytes 4718600 | tf_op jit(solution)/shard_map/ppermute | solution.py:26
  98.6 20.3 %collective-permute-start.14 = (bf16[384,1024]{1,0:T(8,128)(2,1)}, bf16[384,1024]{1,0:T(8,128)(2,1)}, u32[]{:S(2)}, u32[]{:S(2)}) collective-permute-start(bf16[384,1024]{1,0:T(8,128)(2,1)} %add_convert_fusion), channel_id=1, source_target_pairs={{0,4},{1,5},{2,6},{3,7},{4,0},{5,1},{6,2},{7,3},{8,12},{9,13},{10,... | collective-permute-start | bytes 2359304 | tf_op jit(solution)/shard_map/ppermute | solution.py:26
  103.1 22.9 %collective-permute-start.11 = (bf16[384,1024]{1,0:T(8,128)(2,1)}, bf16[384,1024]{1,0:T(8,128)(2,1)}, u32[]{:S(2)}, u32[]{:S(2)}) collective-permute-start(bf16[384,1024]{1,0:T(8,128)(2,1)} %add_convert_fusion.1), channel_id=1, source_target_pairs={{0,2},{1,3},{2,0},{3,1},{4,6},{5,7},{6,4},{7,5},{8,10},{9,11},{10,... | collective-permute-start | bytes 2359304 | tf_op jit(solution)/shard_map/ppermute | solution.py:26
  120.1 11.0 %collective-permute-start.15 = (bf16[192,1024]{1,0:T(8,128)(2,1)S(1)}, bf16[192,1024]{1,0:T(8,128)(2,1)S(1)}, u32[]{:S(2)}, u32[]{:S(2)}) collective-permute-start(bf16[192,1024]{1,0:T(8,128)(2,1)S(1)} %add_convert_fusion.10), channel_id=1, source_target_pairs={{0,2},{1,3},{2,0},{3,1},{4,6},{5,7},{6,4},{7,5},{8,10},{9,11},{10,... | collective-permute-start | bytes 1179656 | tf_op jit(solution)/shard_map/ppermute | solution.py:26
  123.8 28.5 %collective-permute-start.16 = (bf16[512,1024]{1,0:T(8,128)(2,1)}, bf16[512,1024]{1,0:T(8,128)(2,1)S(1)}, u32[]{:S(2)}, u32[]{:S(2)}) collective-permute-start(bf16[512,1024]{1,0:T(8,128)(2,1)} %get-tuple-element.44), channel_id=1, source_target_pairs={{0,8},{8,16},{16,24},{24,0},{1,9},{9,17},{17,25},{25,1},{2,10},{10... | collective-permute-start | bytes 3145736 | tf_op jit(solution)/shard_map/ppermute | solution.py:33
  127.3 9.8 %collective-permute-start.12 = (bf16[192,1024]{1,0:T(8,128)(2,1)S(1)}, bf16[192,1024]{1,0:T(8,128)(2,1)S(1)}, u32[]{:S(2)}, u32[]{:S(2)}) collective-permute-start(bf16[192,1024]{1,0:T(8,128)(2,1)S(1)} %add_convert_fusion.11), channel_id=1, source_target_pairs={{0,4},{1,5},{2,6},{3,7},{4,0},{5,1},{6,2},{7,3},{8,12},{9,13},{10,... | collective-permute-start | bytes 1179656 | tf_op jit(solution)/shard_map/ppermute | solution.py:26
  128.8 50.0 %collective-permute-start.19 = (bf16[512,1024]{1,0:T(8,128)(2,1)}, bf16[512,1024]{1,0:T(8,128)(2,1)}, u32[]{:S(2)}, u32[]{:S(2)}) collective-permute-start(bf16[512,1024]{1,0:T(8,128)(2,1)} %get-tuple-element.44), channel_id=1, source_target_pairs={{0,24},{8,0},{16,8},{24,16},{1,25},{9,1},{17,9},{25,17},{2,26},{10... | collective-permute-start | bytes 3145736 | tf_op jit(solution)/shard_map/ppermute | solution.py:33
  153.7 25.1 %collective-permute-start.17 = (bf16[192,2048]{1,0:T(8,128)(2,1)S(1)}, bf16[192,2048]{1,0:T(8,128)(2,1)}, u32[]{:S(2)}, u32[]{:S(2)}) collective-permute-start(bf16[192,2048]{1,0:T(8,128)(2,1)S(1)} %multiply_convert_fusion.refs_4_), channel_id=1, source_target_pairs={{0,2},{1,3},{2,0},{3,1},{4,6},{5,7},{6,4},{7,5},{8,10},{9,11},{10,... | collective-permute-start | bytes 2359304 | tf_op jit(solution)/shard_map/ppermute | solution.py:26
  154.4 24.5 %collective-permute-start.18 = (bf16[192,2048]{1,0:T(8,128)(2,1)S(1)}, bf16[192,2048]{1,0:T(8,128)(2,1)}, u32[]{:S(2)}, u32[]{:S(2)}) collective-permute-start(bf16[192,2048]{1,0:T(8,128)(2,1)S(1)} %multiply_convert_fusion.refs_4_), channel_id=1, source_target_pairs={{0,4},{1,5},{2,6},{3,7},{4,0},{5,1},{6,2},{7,3},{8,12},{9,13},{10,... | collective-permute-start | bytes 2359304 | tf_op jit(solution)/shard_map/ppermute | solution.py:26
  155.8 48.2 %collective-permute-start.22 = (bf16[192,2048]{1,0:T(8,128)(2,1)S(1)}, bf16[192,2048]{1,0:T(8,128)(2,1)}, u32[]{:S(2)}, u32[]{:S(2)}) collective-permute-start(bf16[192,2048]{1,0:T(8,128)(2,1)S(1)} %multiply_convert_fusion.refs_4_), channel_id=1, source_target_pairs={{0,8},{8,0},{16,24},{24,16},{1,9},{9,1},{17,25},{25,17},{2,10},{10... | collective-permute-start | bytes 2359304 | tf_op jit(solution)/shard_map/ppermute | solution.py:37
  179.9 24.1 %collective-permute-start.20 = (bf16[96,2048]{1,0:T(8,128)(2,1)S(1)}, bf16[96,2048]{1,0:T(8,128)(2,1)}, u32[]{:S(2)}, u32[]{:S(2)}) collective-permute-start(bf16[96,2048]{1,0:T(8,128)(2,1)S(1)} %slice.341), channel_id=1, source_target_pairs={{0,4},{1,5},{2,6},{3,7},{4,0},{5,1},{6,2},{7,3},{8,12},{9,13},{10,... | collective-permute-start | bytes 1179656 | tf_op jit(solution)/shard_map/ppermute | solution.py:26
  181.5 22.5 %collective-permute-start.21 = (bf16[96,2048]{1,0:T(8,128)(2,1)S(1)}, bf16[96,2048]{1,0:T(8,128)(2,1)}, u32[]{:S(2)}, u32[]{:S(2)}) collective-permute-start(bf16[96,2048]{1,0:T(8,128)(2,1)S(1)} %slice.342), channel_id=1, source_target_pairs={{0,2},{1,3},{2,0},{3,1},{4,6},{5,7},{6,4},{7,5},{8,10},{9,11},{10,... | collective-permute-start | bytes 1179656 | tf_op jit(solution)/shard_map/ppermute | solution.py:26
  183.1 44.3 %collective-permute-start.25 = (bf16[512,1024]{1,0:T(8,128)(2,1)S(1)}, bf16[512,1024]{1,0:T(8,128)(2,1)S(1)}, u32[]{:S(2)}, u32[]{:S(2)}) collective-permute-start(bf16[512,1024]{1,0:T(8,128)(2,1)S(1)} %copy-done), channel_id=1, source_target_pairs={{0,16},{8,24},{16,0},{24,8},{1,17},{9,25},{17,1},{25,9},{2,18},{10... | collective-permute-start | bytes 3145736 | tf_op jit(solution)/shard_map/ppermute | solution.py:33
  204.0 27.3 %collective-permute-start.23 = (bf16[192,2048]{1,0:T(8,128)(2,1)}, bf16[192,2048]{1,0:T(8,128)(2,1)}, u32[]{:S(2)}, u32[]{:S(2)}) collective-permute-start(bf16[192,2048]{1,0:T(8,128)(2,1)} %collective-permute-done.22.refs_4_), channel_id=1, source_target_pairs={{0,2},{1,3},{2,0},{3,1},{4,6},{5,7},{6,4},{7,5},{8,10},{9,11},{10,... | collective-permute-start | bytes 2359304 | tf_op jit(solution)/shard_map/ppermute | solution.py:26
  205.2 26.6 %collective-permute-start.24 = (bf16[192,2048]{1,0:T(8,128)(2,1)}, bf16[192,2048]{1,0:T(8,128)(2,1)}, u32[]{:S(2)}, u32[]{:S(2)}) collective-permute-start(bf16[192,2048]{1,0:T(8,128)(2,1)} %collective-permute-done.22.refs_4_), channel_id=1, source_target_pairs={{0,4},{1,5},{2,6},{3,7},{4,0},{5,1},{6,2},{7,3},{8,12},{9,13},{10,... | collective-permute-start | bytes 2359304 | tf_op jit(solution)/shard_map/ppermute | solution.py:26
  205.2 33.2 %collective-permute-start.31 = (bf16[192,2048]{1,0:T(8,128)(2,1)S(1)}, bf16[192,2048]{1,0:T(8,128)(2,1)}, u32[]{:S(2)}, u32[]{:S(2)}) collective-permute-start(bf16[192,2048]{1,0:T(8,128)(2,1)S(1)} %multiply_convert_fusion.refs_4_), channel_id=1, source_target_pairs={{0,1},{1,0},{2,3},{3,2},{4,5},{5,4},{6,7},{7,6},{8,9},{9,8},{10,11... | collective-permute-start | bytes 2359304 | tf_op jit(solution)/shard_map/ppermute | solution.py:26
  205.2 33.6 %collective-permute-start.27 = (bf16[192,2048]{1,0:T(8,128)(2,1)}, bf16[192,2048]{1,0:T(8,128)(2,1)}, u32[]{:S(2)}, u32[]{:S(2)}) collective-permute-start(bf16[192,2048]{1,0:T(8,128)(2,1)} %collective-permute-done.17.refs_0_), channel_id=1, source_target_pairs={{0,1},{1,0},{2,3},{3,2},{4,5},{5,4},{6,7},{7,6},{8,9},{9,8},{10,11... | collective-permute-start | bytes 2359304 | tf_op jit(solution)/shard_map/ppermute | solution.py:26
  228.4 11.4 %collective-permute-start.28 = (bf16[96,2048]{1,0:T(8,128)(2,1)}, bf16[96,2048]{1,0:T(8,128)(2,1)}, u32[]{:S(2)}, u32[]{:S(2)}) collective-permute-start(bf16[96,2048]{1,0:T(8,128)(2,1)} %collective-permute-done.20.refs_1_), channel_id=1, source_target_pairs={{0,1},{1,0},{2,3},{3,2},{4,5},{5,4},{6,7},{7,6},{8,9},{9,8},{10,11... | collective-permute-start | bytes 1179656 | tf_op jit(solution)/shard_map/ppermute | solution.py:26
  231.3 18.5 %collective-permute-start.30 = (bf16[192,2048]{1,0:T(8,128)(2,1)}, bf16[192,2048]{1,0:T(8,128)(2,1)}, u32[]{:S(2)}, u32[]{:S(2)}) collective-permute-start(bf16[192,2048]{1,0:T(8,128)(2,1)} %collective-permute-done.18.refs_3_), channel_id=1, source_target_pairs={{0,1},{1,0},{2,3},{3,2},{4,5},{5,4},{6,7},{7,6},{8,9},{9,8},{10,11... | collective-permute-start | bytes 2359304 | tf_op jit(solution)/shard_map/ppermute | solution.py:26
  231.8 21.8 %collective-permute-start.52 = (bf16[192,2048]{1,0:T(8,128)(2,1)}, bf16[192,2048]{1,0:T(8,128)(2,1)}, u32[]{:S(2)}, u32[]{:S(2)}) collective-permute-start(bf16[192,2048]{1,0:T(8,128)(2,1)} %collective-permute-done.22.refs_4_), channel_id=1, source_target_pairs={{0,1},{1,0},{2,3},{3,2},{4,5},{5,4},{6,7},{7,6},{8,9},{9,8},{10,11... | collective-permute-start | bytes 2359304 | tf_op jit(solution)/shard_map/ppermute | solution.py:26
  238.3 11.3 %collective-permute-start.29 = (bf16[96,2048]{1,0:T(8,128)(2,1)}, bf16[96,2048]{1,0:T(8,128)(2,1)}, u32[]{:S(2)}, u32[]{:S(2)}) collective-permute-start(bf16[96,2048]{1,0:T(8,128)(2,1)} %collective-permute-done.21.refs_2_), channel_id=1, source_target_pairs={{0,1},{1,0},{2,3},{3,2},{4,5},{5,4},{6,7},{7,6},{8,9},{9,8},{10,11... | collective-permute-start | bytes 1179656 | tf_op jit(solution)/shard_map/ppermute | solution.py:26
  238.8 14.8 %collective-permute-start.46 = (bf16[96,2048]{1,0:T(8,128)(2,1)}, bf16[96,2048]{1,0:T(8,128)(2,1)}, u32[]{:S(2)}, u32[]{:S(2)}) collective-permute-start(bf16[96,2048]{1,0:T(8,128)(2,1)} %slice.377), channel_id=1, source_target_pairs={{0,4},{1,5},{2,6},{3,7},{4,0},{5,1},{6,2},{7,3},{8,12},{9,13},{10,... | collective-permute-start | bytes 1179656 | tf_op jit(solution)/shard_map/ppermute | solution.py:26
  239.8 14.3 %collective-permute-start.47 = (bf16[96,2048]{1,0:T(8,128)(2,1)}, bf16[96,2048]{1,0:T(8,128)(2,1)}, u32[]{:S(2)}, u32[]{:S(2)}) collective-permute-start(bf16[96,2048]{1,0:T(8,128)(2,1)} %slice.378), channel_id=1, source_target_pairs={{0,2},{1,3},{2,0},{3,1},{4,6},{5,7},{6,4},{7,5},{8,10},{9,11},{10,... | collective-permute-start | bytes 1179656 | tf_op jit(solution)/shard_map/ppermute | solution.py:26
  249.7 16.9 %collective-permute-start.26 = (bf16[512,512]{1,0:T(8,128)(2,1)S(1)}, bf16[512,512]{1,0:T(8,128)(2,1)S(1)}, u32[]{:S(2)}, u32[]{:S(2)}) collective-permute-start(bf16[512,512]{1,0:T(8,128)(2,1)S(1)} %copy-done.21), channel_id=1, source_target_pairs={{0,8},{8,16},{16,24},{24,0},{1,9},{9,17},{17,25},{25,1},{2,10},{10... | collective-permute-start | bytes 1572872 | tf_op jit(solution)/shard_map/ppermute | solution.py:33
  249.8 24.6 %collective-permute-start.38 = (bf16[512,512]{1,0:T(8,128)(2,1)S(1)}, bf16[512,512]{1,0:T(8,128)(2,1)S(1)}, u32[]{:S(2)}, u32[]{:S(2)}) collective-permute-start(bf16[512,512]{1,0:T(8,128)(2,1)S(1)} %copy-done.21), channel_id=1, source_target_pairs={{0,24},{8,0},{16,8},{24,16},{1,25},{9,1},{17,9},{25,17},{2,26},{10... | collective-permute-start | bytes 1572872 | tf_op jit(solution)/shard_map/ppermute | solution.py:33
  253.6 47.5 %collective-permute-start.48 = (bf16[192,2048]{1,0:T(8,128)(2,1)}, bf16[192,2048]{1,0:T(8,128)(2,1)S(1)}, u32[]{:S(2)}, u32[]{:S(2)}) collective-permute-start(bf16[192,2048]{1,0:T(8,128)(2,1)} %collective-permute-done.23.refs_0_), channel_id=1, source_target_pairs={{0,1},{1,0},{2,3},{3,2},{4,5},{5,4},{6,7},{7,6},{8,9},{9,8},{10,11... | collective-permute-start | bytes 2359304 | tf_op jit(solution)/shard_map/ppermute | solution.py:26
  253.6 50.6 %collective-permute-start.51 = (bf16[192,2048]{1,0:T(8,128)(2,1)}, bf16[192,2048]{1,0:T(8,128)(2,1)S(1)}, u32[]{:S(2)}, u32[]{:S(2)}) collective-permute-start(bf16[192,2048]{1,0:T(8,128)(2,1)} %collective-permute-done.24.refs_3_), channel_id=1, source_target_pairs={{0,1},{1,0},{2,3},{3,2},{4,5},{5,4},{6,7},{7,6},{8,9},{9,8},{10,11... | collective-permute-start | bytes 2359304 | tf_op jit(solution)/shard_map/ppermute | solution.py:26
  254.1 44.0 %collective-permute-start.39 = (bf16[512,512]{1,0:T(8,128)(2,1)S(1)}, bf16[512,512]{1,0:T(8,128)(2,1)S(1)}, u32[]{:S(2)}, u32[]{:S(2)}) collective-permute-start(bf16[512,512]{1,0:T(8,128)(2,1)S(1)} %copy-done.3), channel_id=1, source_target_pairs={{0,16},{8,24},{16,0},{24,8},{1,17},{9,25},{17,1},{25,9},{2,18},{10... | collective-permute-start | bytes 1572872 | tf_op jit(solution)/shard_map/ppermute | solution.py:33
  266.6 37.1 %collective-permute-start.49 = (bf16[96,2048]{1,0:T(8,128)(2,1)}, bf16[96,2048]{1,0:T(8,128)(2,1)S(1)}, u32[]{:S(2)}, u32[]{:S(2)}) collective-permute-start(bf16[96,2048]{1,0:T(8,128)(2,1)} %collective-permute-done.46.refs_1_), channel_id=1, source_target_pairs={{0,1},{1,0},{2,3},{3,2},{4,5},{5,4},{6,7},{7,6},{8,9},{9,8},{10,11... | collective-permute-start | bytes 1179656 | tf_op jit(solution)/shard_map/ppermute | solution.py:26
  274.4 29.3 %collective-permute-start.50 = (bf16[96,2048]{1,0:T(8,128)(2,1)}, bf16[96,2048]{1,0:T(8,128)(2,1)S(1)}, u32[]{:S(2)}, u32[]{:S(2)}) collective-permute-start(bf16[96,2048]{1,0:T(8,128)(2,1)} %collective-permute-done.47.refs_2_), channel_id=1, source_target_pairs={{0,1},{1,0},{2,3},{3,2},{4,5},{5,4},{6,7},{7,6},{8,9},{9,8},{10,11... | collective-permute-start | bytes 1179656 | tf_op jit(solution)/shard_map/ppermute | solution.py:26
  298.1 13.9 %collective-permute-start.32 = (bf16[768,512]{1,0:T(8,128)(2,1)S(1)}, bf16[768,512]{1,0:T(8,128)(2,1)S(1)}, u32[]{:S(2)}, u32[]{:S(2)}) collective-permute-start(bf16[768,512]{1,0:T(8,128)(2,1)S(1)} %get-tuple-element.56), channel_id=1, source_target_pairs={{0,1},{1,0},{2,3},{3,2},{4,5},{5,4},{6,7},{7,6},{8,9},{9,8},{10,11... | collective-permute-start | bytes 2359304 | tf_op jit(solution)/shard_map/ppermute | solution.py:26
  301.1 11.5 %collective-permute-start.35 = (bf16[768,512]{1,0:T(8,128)(2,1)S(1)}, bf16[768,512]{1,0:T(8,128)(2,1)S(1)}, u32[]{:S(2)}, u32[]{:S(2)}) collective-permute-start(bf16[768,512]{1,0:T(8,128)(2,1)S(1)} %get-tuple-element.58), channel_id=1, source_target_pairs={{0,1},{1,0},{2,3},{3,2},{4,5},{5,4},{6,7},{7,6},{8,9},{9,8},{10,11... | collective-permute-start | bytes 2359304 | tf_op jit(solution)/shard_map/ppermute | solution.py:26
  303.6 9.2 %collective-permute-start.40 = (bf16[768,512]{1,0:T(8,128)(2,1)S(1)}, bf16[768,512]{1,0:T(8,128)(2,1)S(1)}, u32[]{:S(2)}, u32[]{:S(2)}) collective-permute-start(bf16[768,512]{1,0:T(8,128)(2,1)S(1)} %get-tuple-element.60), channel_id=1, source_target_pairs={{0,1},{1,0},{2,3},{3,2},{4,5},{5,4},{6,7},{7,6},{8,9},{9,8},{10,11... | collective-permute-start | bytes 2359304 | tf_op jit(solution)/shard_map/ppermute | solution.py:26
  303.7 9.7 %collective-permute-start.43 = (bf16[768,512]{1,0:T(8,128)(2,1)S(1)}, bf16[768,512]{1,0:T(8,128)(2,1)S(1)}, u32[]{:S(2)}, u32[]{:S(2)}) collective-permute-start(bf16[768,512]{1,0:T(8,128)(2,1)S(1)} %get-tuple-element.62), channel_id=1, source_target_pairs={{0,1},{1,0},{2,3},{3,2},{4,5},{5,4},{6,7},{7,6},{8,9},{9,8},{10,11... | collective-permute-start | bytes 2359304 | tf_op jit(solution)/shard_map/ppermute | solution.py:26
  313.5 12.0 %collective-permute-start.33 = (bf16[384,512]{1,0:T(8,128)(2,1)S(1)}, bf16[384,512]{1,0:T(8,128)(2,1)S(1)}, u32[]{:S(2)}, u32[]{:S(2)}) collective-permute-start(bf16[384,512]{1,0:T(8,128)(2,1)S(1)} %add_convert_fusion.9), channel_id=1, source_target_pairs={{0,2},{1,3},{2,0},{3,1},{4,6},{5,7},{6,4},{7,5},{8,10},{9,11},{10,... | collective-permute-start | bytes 1179656 | tf_op jit(solution)/shard_map/ppermute | solution.py:26
  314.6 12.1 %collective-permute-start.36 = (bf16[384,512]{1,0:T(8,128)(2,1)S(1)}, bf16[384,512]{1,0:T(8,128)(2,1)S(1)}, u32[]{:S(2)}, u32[]{:S(2)}) collective-permute-start(bf16[384,512]{1,0:T(8,128)(2,1)S(1)} %add_convert_fusion.8), channel_id=1, source_target_pairs={{0,4},{1,5},{2,6},{3,7},{4,0},{5,1},{6,2},{7,3},{8,12},{9,13},{10,... | collective-permute-start | bytes 1179656 | tf_op jit(solution)/shard_map/ppermute | solution.py:26
  316.4 17.5 %collective-permute-start.41 = (bf16[384,512]{1,0:T(8,128)(2,1)S(1)}, bf16[384,512]{1,0:T(8,128)(2,1)S(1)}, u32[]{:S(2)}, u32[]{:S(2)}) collective-permute-start(bf16[384,512]{1,0:T(8,128)(2,1)S(1)} %add_convert_fusion.7), channel_id=1, source_target_pairs={{0,2},{1,3},{2,0},{3,1},{4,6},{5,7},{6,4},{7,5},{8,10},{9,11},{10,... | collective-permute-start | bytes 1179656 | tf_op jit(solution)/shard_map/ppermute | solution.py:26
  317.7 17.4 %collective-permute-start.44 = (bf16[384,512]{1,0:T(8,128)(2,1)S(1)}, bf16[384,512]{1,0:T(8,128)(2,1)S(1)}, u32[]{:S(2)}, u32[]{:S(2)}) collective-permute-start(bf16[384,512]{1,0:T(8,128)(2,1)S(1)} %add_convert_fusion.6), channel_id=1, source_target_pairs={{0,4},{1,5},{2,6},{3,7},{4,0},{5,1},{6,2},{7,3},{8,12},{9,13},{10,... | collective-permute-start | bytes 1179656 | tf_op jit(solution)/shard_map/ppermute | solution.py:26
  318.2 49.3 %collective-permute-start.57 = (bf16[384,512]{1,0:T(8,128)(2,1)S(1)}, bf16[384,512]{1,0:T(8,128)(2,1)S(1)}, u32[]{:S(2)}, u32[]{:S(2)}) collective-permute-start(bf16[384,512]{1,0:T(8,128)(2,1)S(1)} %add_convert_fusion.4), channel_id=1, source_target_pairs={{0,4},{1,5},{2,6},{3,7},{4,0},{5,1},{6,2},{7,3},{8,12},{9,13},{10,... | collective-permute-start | bytes 1179656 | tf_op jit(solution)/shard_map/ppermute | solution.py:26
  325.5 43.1 %collective-permute-start.54 = (bf16[384,512]{1,0:T(8,128)(2,1)S(1)}, bf16[384,512]{1,0:T(8,128)(2,1)S(1)}, u32[]{:S(2)}, u32[]{:S(2)}) collective-permute-start(bf16[384,512]{1,0:T(8,128)(2,1)S(1)} %add_convert_fusion.5), channel_id=1, source_target_pairs={{0,2},{1,3},{2,0},{3,1},{4,6},{5,7},{6,4},{7,5},{8,10},{9,11},{10,... | collective-permute-start | bytes 1179656 | tf_op jit(solution)/shard_map/ppermute | solution.py:26
  326.6 43.8 %collective-permute-start.64 = (bf16[384,512]{1,0:T(8,128)(2,1)S(1)}, bf16[384,512]{1,0:T(8,128)(2,1)S(1)}, u32[]{:S(2)}, u32[]{:S(2)}) collective-permute-start(bf16[384,512]{1,0:T(8,128)(2,1)S(1)} %add_convert_fusion.2), channel_id=1, source_target_pairs={{0,4},{1,5},{2,6},{3,7},{4,0},{5,1},{6,2},{7,3},{8,12},{9,13},{10,... | collective-permute-start | bytes 1179656 | tf_op jit(solution)/shard_map/ppermute | solution.py:26
  333.9 37.8 %collective-permute-start.61 = (bf16[384,512]{1,0:T(8,128)(2,1)S(1)}, bf16[384,512]{1,0:T(8,128)(2,1)S(1)}, u32[]{:S(2)}, u32[]{:S(2)}) collective-permute-start(bf16[384,512]{1,0:T(8,128)(2,1)S(1)} %add_convert_fusion.3), channel_id=1, source_target_pairs={{0,2},{1,3},{2,0},{3,1},{4,6},{5,7},{6,4},{7,5},{8,10},{9,11},{10,... | collective-permute-start | bytes 1179656 | tf_op jit(solution)/shard_map/ppermute | solution.py:26
  335.1 19.9 %collective-permute-start.34 = (bf16[192,512]{1,0:T(8,128)(2,1)S(1)}, bf16[192,512]{1,0:T(8,128)(2,1)S(1)}, u32[]{:S(2)}, u32[]{:S(2)}) collective-permute-start(bf16[192,512]{1,0:T(8,128)(2,1)S(1)} %add_convert_fusion.23), channel_id=1, source_target_pairs={{0,4},{1,5},{2,6},{3,7},{4,0},{5,1},{6,2},{7,3},{8,12},{9,13},{10,... | collective-permute-start | bytes 589832 | tf_op jit(solution)/shard_map/ppermute | solution.py:26
  354.9 5.7 %collective-permute-start.37 = (bf16[192,512]{1,0:T(8,128)(2,1)S(1)}, bf16[192,512]{1,0:T(8,128)(2,1)S(1)}, u32[]{:S(2)}, u32[]{:S(2)}) collective-permute-start(bf16[192,512]{1,0:T(8,128)(2,1)S(1)} %add_convert_fusion.22), channel_id=1, source_target_pairs={{0,2},{1,3},{2,0},{3,1},{4,6},{5,7},{6,4},{7,5},{8,10},{9,11},{10,... | collective-permute-start | bytes 589832 | tf_op jit(solution)/shard_map/ppermute | solution.py:26
  360.7 5.7 %collective-permute-start.42 = (bf16[192,512]{1,0:T(8,128)(2,1)S(1)}, bf16[192,512]{1,0:T(8,128)(2,1)S(1)}, u32[]{:S(2)}, u32[]{:S(2)}) collective-permute-start(bf16[192,512]{1,0:T(8,128)(2,1)S(1)} %add_convert_fusion.21), channel_id=1, source_target_pairs={{0,4},{1,5},{2,6},{3,7},{4,0},{5,1},{6,2},{7,3},{8,12},{9,13},{10,... | collective-permute-start | bytes 589832 | tf_op jit(solution)/shard_map/ppermute | solution.py:26
  366.4 12.4 %collective-permute-start.45 = (bf16[192,512]{1,0:T(8,128)(2,1)S(1)}, bf16[192,512]{1,0:T(8,128)(2,1)S(1)}, u32[]{:S(2)}, u32[]{:S(2)}) collective-permute-start(bf16[192,512]{1,0:T(8,128)(2,1)S(1)} %add_convert_fusion.20), channel_id=1, source_target_pairs={{0,2},{1,3},{2,0},{3,1},{4,6},{5,7},{6,4},{7,5},{8,10},{9,11},{10,... | collective-permute-start | bytes 589832 | tf_op jit(solution)/shard_map/ppermute | solution.py:26
  367.7 8.4 %collective-permute-start.58 = (bf16[192,512]{1,0:T(8,128)(2,1)S(1)}, bf16[192,512]{1,0:T(8,128)(2,1)S(1)}, u32[]{:S(2)}, u32[]{:S(2)}) collective-permute-start(bf16[192,512]{1,0:T(8,128)(2,1)S(1)} %add_convert_fusion.17), channel_id=1, source_target_pairs={{0,2},{1,3},{2,0},{3,1},{4,6},{5,7},{6,4},{7,5},{8,10},{9,11},{10,... | collective-permute-start | bytes 589832 | tf_op jit(solution)/shard_map/ppermute | solution.py:26
  368.7 7.4 %collective-permute-start.55 = (bf16[192,512]{1,0:T(8,128)(2,1)S(1)}, bf16[192,512]{1,0:T(8,128)(2,1)S(1)}, u32[]{:S(2)}, u32[]{:S(2)}) collective-permute-start(bf16[192,512]{1,0:T(8,128)(2,1)S(1)} %add_convert_fusion.19), channel_id=1, source_target_pairs={{0,4},{1,5},{2,6},{3,7},{4,0},{5,1},{6,2},{7,3},{8,12},{9,13},{10,... | collective-permute-start | bytes 589832 | tf_op jit(solution)/shard_map/ppermute | solution.py:26
  370.5 7.6 %collective-permute-start.65 = (bf16[192,512]{1,0:T(8,128)(2,1)S(1)}, bf16[192,512]{1,0:T(8,128)(2,1)S(1)}, u32[]{:S(2)}, u32[]{:S(2)}) collective-permute-start(bf16[192,512]{1,0:T(8,128)(2,1)S(1)} %add_convert_fusion.13), channel_id=1, source_target_pairs={{0,2},{1,3},{2,0},{3,1},{4,6},{5,7},{6,4},{7,5},{8,10},{9,11},{10,... | collective-permute-start | bytes 589832 | tf_op jit(solution)/shard_map/ppermute | solution.py:26
  371.8 6.5 %collective-permute-start.62 = (bf16[192,512]{1,0:T(8,128)(2,1)S(1)}, bf16[192,512]{1,0:T(8,128)(2,1)S(1)}, u32[]{:S(2)}, u32[]{:S(2)}) collective-permute-start(bf16[192,512]{1,0:T(8,128)(2,1)S(1)} %add_convert_fusion.15), channel_id=1, source_target_pairs={{0,4},{1,5},{2,6},{3,7},{4,0},{5,1},{6,2},{7,3},{8,12},{9,13},{10,... | collective-permute-start | bytes 589832 | tf_op jit(solution)/shard_map/ppermute | solution.py:26
  376.3 8.8 %collective-permute-start.59 = (bf16[192,1024]{1,0:T(8,128)(2,1)S(1)}, bf16[192,1024]{1,0:T(8,128)(2,1)S(1)}, u32[]{:S(2)}, u32[]{:S(2)}) collective-permute-start(bf16[192,1024]{1,0:T(8,128)(2,1)S(1)} %pad_maximum_fusion.8), channel_id=1, source_target_pairs={{0,8},{8,0},{16,24},{24,16},{1,9},{9,1},{17,25},{25,17},{2,10},{10... | collective-permute-start | bytes 1179656 | tf_op jit(solution)/shard_map/ppermute | solution.py:37
  378.4 10.9 %collective-permute-start.66 = (bf16[192,1024]{1,0:T(8,128)(2,1)S(1)}, bf16[192,1024]{1,0:T(8,128)(2,1)S(1)}, u32[]{:S(2)}, u32[]{:S(2)}) collective-permute-start(bf16[192,1024]{1,0:T(8,128)(2,1)S(1)} %pad_maximum_fusion.9), channel_id=1, source_target_pairs={{0,8},{8,0},{16,24},{24,16},{1,9},{9,1},{17,25},{25,17},{2,10},{10... | collective-permute-start | bytes 1179656 | tf_op jit(solution)/shard_map/ppermute | solution.py:37
  (34 other events, 245.7 us)
Sparse Core Ops, SparseCore 0:
  11.3 48.6 all-gather.2
  61.6 29.3 all-gather.4
